TPU v7x, 32 devices: a whole 2x2x4 slice. The times are simulated.
32 devices in a mesh: section: 2 (over core), region: 16 (over z, y, x).
Axes of the slice: x: 2, y: 2, z: 4, core: 2. Of those that a mesh axis runs over, the one named last changes fastest.
Arguments:
- hits: bfloat16 [2, 4096, 512], P('section', 'region'), may hold values from -6 to 6
- order: int32 [2, 16, 256], P(None, 'region'), may hold values from 0 to 255, each once within a row
- links: int32 [2, 32, 3], P(None, 'region'), may hold values from 0 to 31, as said below
- counts: int32 [2, 16], replicated, may hold values from 64 to 256, as said below
- w_qkv: bfloat16 [2, 512, 1536], P('section')
- w_out: bfloat16 [2, 512, 512], P('section'), may hold values from -0.25 to 0.25
- w_up: bfloat16 [2, 512, 2048], P('section'), may hold values from -0.25 to 0.25
- w_down: bfloat16 [2, 2048, 512], P('section'), may hold values from -0.125 to 0.125
Outputs:
- encoded: bfloat16 [2, 4096, 512], P('section', 'region')
Inputs may be any that keep to these rules, and one draw needn't show every extreme that they name: `links`: entry 0 of patch g is g itself; the other entries are distinct patches other than g, at most 2 patches away from g along the curve. `counts`: in every event some region is full and some region holds 64 hits. `order`: each region's entries along the last dimension list each of its 256 hits once.
All inputs are finite; a program needn't handle non-finite values.
Results may differ from a plain program's by a relative error of at most 0.015.
Values may be sent and summed in bfloat16 or wider, within the bound.
A program may use at most 64 MiB of HBM per device.

v0:
```python
import jax
import jax.numpy as jnp
from jax import lax
from jax.sharding import PartitionSpec as P

HEADS = 8
REACH = 2


epsilon = 1e-05


def with_halo(cells, sides, width):
    for axis, dim in sides:
        count = lax.axis_size(axis)
        ends = count - 1
        head = lax.slice_in_dim(cells, 0, width, axis=dim)
        tail = lax.slice_in_dim(cells, cells.shape[dim] - width, cells.shape[dim], axis=dim)
        cells = jnp.concatenate(
            [
                lax.ppermute(tail, axis, [(i, (i + 1) % count) for i in range(ends)]),
                cells,
                lax.ppermute(head, axis, [((i + 1) % count, i) for i in range(ends)]),
            ],
            axis=dim,
        )
    return cells


def passed_along(value, axis, by):
    size = lax.axis_size(axis)
    pairs = [(i, i + by) for i in range(size) if 0 <= i + by < size]
    return lax.ppermute(value, axis, pairs)


def normalize(state):
    values = state.astype(jnp.float32)
    center = jnp.mean(values, axis=-1, keepdims=True)
    spread = jnp.mean((values - center) ** 2, axis=-1, keepdims=True)
    return ((values - center) * lax.rsqrt(spread + epsilon)).astype(jnp.bfloat16)


def attend(queries, near_keys, near_values, key_valid, local_links, patch_rows):
    patch_count = local_links.shape[0]
    links_count = local_links.shape[1]
    feature_width = queries.shape[1]
    head_width = feature_width // HEADS
    query_part = queries.reshape(patch_count, patch_rows, HEADS, head_width)
    key_part = near_keys.reshape(-1, patch_rows, HEADS, head_width)[local_links]
    key_part = key_part.reshape(patch_count, links_count * patch_rows, HEADS, head_width)
    value_part = near_values.reshape(-1, patch_rows, HEADS, head_width)[local_links]
    value_part = value_part.reshape(patch_count, links_count * patch_rows, HEADS, head_width)
    key_mask = key_valid.reshape(-1, patch_rows)[local_links].reshape(
        patch_count, links_count * patch_rows
    )
    scores = jnp.einsum(
        "pqhd,pkhd->phqk", query_part, key_part, preferred_element_type=jnp.float32
    ) * head_width ** (-0.5)
    scores = jnp.where(key_mask[:, None, None, :], scores, -1e30)
    highest = jnp.max(scores, axis=-1, keepdims=True)
    weights = jnp.exp(scores - highest)
    probs = (weights / jnp.sum(weights, axis=-1, keepdims=True)).astype(jnp.bfloat16)
    output = jnp.einsum("phqk,pkhd->pqhd", probs, value_part, preferred_element_type=jnp.float32)
    return output.reshape(patch_count * patch_rows, feature_width).astype(jnp.bfloat16)


def per_device(hits, order, links, counts, w_qkv, w_out, w_up, w_down):
    segments = lax.axis_size("section")
    segment_index = lax.axis_index("section")
    region_index = lax.axis_index("region")
    row_count = hits.shape[1]
    feature_width = hits.shape[2]
    patch_count = links.shape[1]
    patch_rows = row_count // patch_count
    margin = REACH * patch_rows
    region_total = counts.shape[1]
    slot_ids = jnp.arange(row_count + 2 * margin)
    place = region_index * row_count - margin + slot_ids
    owner = place // row_count
    inside = (place >= 0) & (place < region_total * row_count)
    offset = place - owner * row_count
    region_ids = jnp.arange(region_total)

    def run_block(state, event_index):
        count_row = counts[event_index]
        key_count = jnp.sum(
            jnp.where(owner[:, None] == region_ids[None, :], count_row[None, :], 0), axis=1
        )
        key_valid = inside & (offset < key_count)
        local_links = links[event_index] - region_index * patch_count + REACH
        weight_qkv = w_qkv[0]
        normed = normalize(state)
        wide_normed = with_halo(normed, (("region", 0),), margin)
        queries = jnp.dot(
            normed, weight_qkv[:, :feature_width], preferred_element_type=jnp.float32
        ).astype(jnp.bfloat16)
        paired = jnp.dot(
            wide_normed, weight_qkv[:, feature_width:], preferred_element_type=jnp.float32
        ).astype(jnp.bfloat16)
        near_keys = paired[:, :feature_width]
        near_values = paired[:, feature_width:]
        attended = attend(queries, near_keys, near_values, key_valid, local_links, patch_rows)
        middle = (
            state.astype(jnp.float32)
            + jnp.dot(attended, w_out[0], preferred_element_type=jnp.float32)
        ).astype(jnp.bfloat16)
        normed_mlp = normalize(middle)
        hidden = jax.nn.gelu(
            jnp.dot(normed_mlp, w_up[0], preferred_element_type=jnp.float32), approximate=False
        ).astype(jnp.bfloat16)
        state = (
            middle.astype(jnp.float32)
            + jnp.dot(hidden, w_down[0], preferred_element_type=jnp.float32)
        ).astype(jnp.bfloat16)
        return state

    every_event = lax.all_gather(hits, "section", axis=0, tiled=True)
    collected = jnp.zeros((segments, row_count, feature_width), jnp.bfloat16)

    def step_once(tick_index, carry):
        state, gathered_out = carry
        event_index = jnp.clip(tick_index - segment_index, 0, segments - 1)
        fresh = lax.dynamic_index_in_dim(
            every_event, jnp.minimum(tick_index, segments - 1), 0, keepdims=False
        )
        arranged = fresh[order[event_index, 0]]
        current = jnp.where(segment_index == 0, arranged, state)
        result = run_block(current, event_index)
        passed = passed_along(result, "section", 1)
        gathered_out = lax.dynamic_update_index_in_dim(gathered_out, result, event_index, 0)
        return (passed, gathered_out)

    start_state = jnp.zeros((row_count, feature_width), jnp.bfloat16)
    final_carry = lax.fori_loop(0, 2 * segments - 1, step_once, (start_state, collected))
    finished = final_carry[1]
    spread_out = lax.all_to_all(finished, "section", split_axis=0, concat_axis=0, tiled=True)
    final_rows = spread_out[segments - 1]
    own_count = counts[segment_index, region_index]
    keep_rows = jnp.arange(row_count) < own_count
    return jnp.where(keep_rows[:, None], final_rows, jnp.zeros_like(final_rows))[None]


def solution(mesh):
    in_specs = (
        P("section", "region", None),
        P(None, "region", None),
        P(None, "region", None),
        P(),
        P("section", None, None),
        P("section", None, None),
        P("section", None, None),
        P("section", None, None),
    )
    out_specs = P("section", "region", None)
    return jax.shard_map(
        per_device, mesh=mesh, in_specs=in_specs, out_specs=out_specs, check_vma=False
    )
```

profile of v0, /device:TPU:24, one launch (start us, length us, event | category | flops | bytes accessed | tf_op | source)
XLA Modules:
  0.0 141.3 jit_solution(15828110564109526325)
XLA Ops:
  0.0 2.4 %all_gather.3 = bf16[2,256,512]{2,1,0:T(8,128)(2,1)S(1)} all-gather(bf16[1,256,512]{2,1,0:T(8,128)(2,1)} %param.10), channel_id=1, replica_groups=mesh['section'=2,'region'=16] {'section'}, dimensions={0}, use_global_device_ids=true | all-gather | bytes 786432 | tf_op jit(solution)/shard_map/all_gather | solution.py:117
  3.2 131.8 %while.19 = (s32[]{:T(128)}, bf16[256,512]{1,0:T(8,128)(2,1)S(1)}, bf16[2,256,512]{2,1,0:T(8,128)(2,1)}, pred[]{:T(512)}, bf16[2,256,512]{2,1,0:T(8,128)(2,1)S(1...) while((s32[]{:T(128)}, bf16[256,512]{1,0:T(8,128)(2,1)S(1)}, ...), condition=%wide.region_8.9_spmd.clone.clone, body=%wide.region_0.8_spmd.clone.clone.sunk | while | flops 2395803648 | bytes 76874000 | solution.py:134
  5.7 3.4 %collective-permute-start.1 = (bf16[256,512]{1,0:T(8,128)(2,1)S(1)}, bf16[256,512]{1,0:T(8,128)(2,1)S(1)}, u32[]{:S(2)}, u32[]{:S(2)}) collective-permute-start(bf16[256,512]{1,0:T(8,128)(2,1)S(1)} %fusion.177), channel_id=1, source_target_pairs={{0,1},{1,2},{2,3},{3,4},{4,5},{5,6},{6,7},{7,8},{8,9},{9,10},{10,1... | collective-permute-start | bytes 786440 | tf_op jit(solution)/shard_map/while/body/eval_jaxpr/ppermute | solution.py:21
  9.1 4.2 %collective-permute-start = (bf16[256,512]{1,0:T(8,128)(2,1)S(1)}, bf16[256,512]{1,0:T(8,128)(2,1)S(1)}, u32[]{:S(2)}, u32[]{:S(2)}) collective-permute-start(bf16[256,512]{1,0:T(8,128)(2,1)S(1)} %fusion.177), channel_id=1, source_target_pairs={{1,0},{2,1},{3,2},{4,3},{5,4},{6,5},{7,6},{8,7},{9,8},{10,9},{11,1... | collective-permute-start | bytes 786440 | tf_op jit(solution)/shard_map/while/body/eval_jaxpr/ppermute | solution.py:23
  15.6 2.2 %collective-permute-done.1 = bf16[256,512]{1,0:T(8,128)(2,1)S(1)} collective-permute-done((bf16[256,512]{1,0:T(8,128)(2,1)S(1)}, bf16[256,512]{1,0:T(8,128)(2,1)S(1)}, u32[]{:S(2)}, u32[]{:S(2)}) %collective-permute-start.1) | collective-permute-done | bytes 262176 | tf_op jit(solution)/shard_map/while/body/eval_jaxpr/ppermute | solution.py:21
  17.8 4.7 %collective-permute-done = bf16[256,512]{1,0:T(8,128)(2,1)S(1)} collective-permute-done((bf16[256,512]{1,0:T(8,128)(2,1)S(1)}, bf16[256,512]{1,0:T(8,128)(2,1)S(1)}, u32[]{:S(2)}, u32[]{:S(2)}) %collective-permute-start) | collective-permute-done | bytes 262176 | tf_op jit(solution)/shard_map/while/body/eval_jaxpr/ppermute | solution.py:23
  27.5 1.5 %reshape.302 = bf16[2,384,8,64]{1,0,3,2:T(2,128)(2,1)} reshape(bf16[6,128,8,64]{1,0,3,2:T(8,128)(2,1)S(1)} %copy.83) | data formatting | bytes 1572864 | tf_op jit(solution)/shard_map/while/body/eval_jaxpr/reshape | solution.py:50
  36.5 7.8 %bitcast_dynamic-update-slice_fusion.2 = (bf16[2,256,512]{2,1,0:T(8,128)(2,1)S(1)}, bf16[256,512]{1,0:T(8,128)(2,1)S(1)}) fusion(bf16[2,256,512]{2,1,0:T(8,128)(2,1)S(1)} %copy-done.6, s32[]{:T(128)S(6)} %min.27, f32[256,512]{1,0:T(8,128)S(1)} %get-tuple-element.635, bf16[1,2048,512]{2,1,0:T(8,128)(2,1)} %get-tuple-element.688, ...), kind=kOutput, calls=%fused_computation.101.clone.1 | convolution fusion | flops 1108475904 | bytes 5769220 | tf_op jit(solution)/shard_map/while/body/eval_jaxpr/dot_general | solution.py:113
  44.3 1.3 collective-permute-start.2
  49.2 3.4 %collective-permute-start.1 = (bf16[256,512]{1,0:T(8,128)(2,1)S(1)}, bf16[256,512]{1,0:T(8,128)(2,1)S(1)}, u32[]{:S(2)}, u32[]{:S(2)}) collective-permute-start(bf16[256,512]{1,0:T(8,128)(2,1)S(1)} %fusion.177), channel_id=1, source_target_pairs={{0,1},{1,2},{2,3},{3,4},{4,5},{5,6},{6,7},{7,8},{8,9},{9,10},{10,1... | collective-permute-start | bytes 786440 | tf_op jit(solution)/shard_map/while/body/eval_jaxpr/ppermute | solution.py:21
  52.7 4.2 %collective-permute-start = (bf16[256,512]{1,0:T(8,128)(2,1)S(1)}, bf16[256,512]{1,0:T(8,128)(2,1)S(1)}, u32[]{:S(2)}, u32[]{:S(2)}) collective-permute-start(bf16[256,512]{1,0:T(8,128)(2,1)S(1)} %fusion.177), channel_id=1, source_target_pairs={{1,0},{2,1},{3,2},{4,3},{5,4},{6,5},{7,6},{8,7},{9,8},{10,9},{11,1... | collective-permute-start | bytes 786440 | tf_op jit(solution)/shard_map/while/body/eval_jaxpr/ppermute | solution.py:23
  59.1 2.5 %collective-permute-done.1 = bf16[256,512]{1,0:T(8,128)(2,1)S(1)} collective-permute-done((bf16[256,512]{1,0:T(8,128)(2,1)S(1)}, bf16[256,512]{1,0:T(8,128)(2,1)S(1)}, u32[]{:S(2)}, u32[]{:S(2)}) %collective-permute-start.1) | collective-permute-done | bytes 262176 | tf_op jit(solution)/shard_map/while/body/eval_jaxpr/ppermute | solution.py:21
  61.6 5.2 %collective-permute-done = bf16[256,512]{1,0:T(8,128)(2,1)S(1)} collective-permute-done((bf16[256,512]{1,0:T(8,128)(2,1)S(1)}, bf16[256,512]{1,0:T(8,128)(2,1)S(1)}, u32[]{:S(2)}, u32[]{:S(2)}) %collective-permute-start) | collective-permute-done | bytes 262176 | tf_op jit(solution)/shard_map/while/body/eval_jaxpr/ppermute | solution.py:23
  71.8 1.5 %reshape.302 = bf16[2,384,8,64]{1,0,3,2:T(2,128)(2,1)} reshape(bf16[6,128,8,64]{1,0,3,2:T(8,128)(2,1)S(1)} %copy.83) | data formatting | bytes 1572864 | tf_op jit(solution)/shard_map/while/body/eval_jaxpr/reshape | solution.py:50
  80.8 7.8 %bitcast_dynamic-update-slice_fusion.2 = (bf16[2,256,512]{2,1,0:T(8,128)(2,1)S(1)}, bf16[256,512]{1,0:T(8,128)(2,1)S(1)}) fusion(bf16[2,256,512]{2,1,0:T(8,128)(2,1)S(1)} %copy-done.6, s32[]{:T(128)S(6)} %min.27, f32[256,512]{1,0:T(8,128)S(1)} %get-tuple-element.635, bf16[1,2048,512]{2,1,0:T(8,128)(2,1)} %get-tuple-element.688, ...), kind=kOutput, calls=%fused_computation.101.clone.1 | convolution fusion | flops 1108475904 | bytes 5769220 | tf_op jit(solution)/shard_map/while/body/eval_jaxpr/dot_general | solution.py:113
  88.6 1.5 %collective-permute-start.2 = (bf16[256,512]{1,0:T(8,128)(2,1)S(1)}, bf16[256,512]{1,0:T(8,128)(2,1)S(1)}, u32[]{:S(2)}, u32[]{:S(2)}) collective-permute-start(bf16[256,512]{1,0:T(8,128)(2,1)S(1)} %get-tuple-element.637), channel_id=1, source_target_pairs={{0,16},{1,17},{2,18},{3,19},{4,20},{5,21},{6,22},{7,23},{8,24},{9,... | collective-permute-start | bytes 786440 | tf_op jit(solution)/shard_map/while/body/eval_jaxpr/ppermute | solution.py:33
  93.7 2.5 %collective-permute-start.1 = (bf16[256,512]{1,0:T(8,128)(2,1)S(1)}, bf16[256,512]{1,0:T(8,128)(2,1)S(1)}, u32[]{:S(2)}, u32[]{:S(2)}) collective-permute-start(bf16[256,512]{1,0:T(8,128)(2,1)S(1)} %fusion.177), channel_id=1, source_target_pairs={{0,1},{1,2},{2,3},{3,4},{4,5},{5,6},{6,7},{7,8},{8,9},{9,10},{10,1... | collective-permute-start | bytes 786440 | tf_op jit(solution)/shard_map/while/body/eval_jaxpr/ppermute | solution.py:21
  96.1 5.2 %collective-permute-start = (bf16[256,512]{1,0:T(8,128)(2,1)S(1)}, bf16[256,512]{1,0:T(8,128)(2,1)S(1)}, u32[]{:S(2)}, u32[]{:S(2)}) collective-permute-start(bf16[256,512]{1,0:T(8,128)(2,1)S(1)} %fusion.177), channel_id=1, source_target_pairs={{1,0},{2,1},{3,2},{4,3},{5,4},{6,5},{7,6},{8,7},{9,8},{10,9},{11,1... | collective-permute-start | bytes 786440 | tf_op jit(solution)/shard_map/while/body/eval_jaxpr/ppermute | solution.py:23
  103.6 2.5 %collective-permute-done.1 = bf16[256,512]{1,0:T(8,128)(2,1)S(1)} collective-permute-done((bf16[256,512]{1,0:T(8,128)(2,1)S(1)}, bf16[256,512]{1,0:T(8,128)(2,1)S(1)}, u32[]{:S(2)}, u32[]{:S(2)}) %collective-permute-start.1) | collective-permute-done | bytes 262176 | tf_op jit(solution)/shard_map/while/body/eval_jaxpr/ppermute | solution.py:21
  106.1 4.5 %collective-permute-done = bf16[256,512]{1,0:T(8,128)(2,1)S(1)} collective-permute-done((bf16[256,512]{1,0:T(8,128)(2,1)S(1)}, bf16[256,512]{1,0:T(8,128)(2,1)S(1)}, u32[]{:S(2)}, u32[]{:S(2)}) %collective-permute-start) | collective-permute-done | bytes 262176 | tf_op jit(solution)/shard_map/while/body/eval_jaxpr/ppermute | solution.py:23
  115.6 1.5 %reshape.302 = bf16[2,384,8,64]{1,0,3,2:T(2,128)(2,1)} reshape(bf16[6,128,8,64]{1,0,3,2:T(8,128)(2,1)S(1)} %copy.83) | data formatting | bytes 1572864 | tf_op jit(solution)/shard_map/while/body/eval_jaxpr/reshape | solution.py:50
  124.6 7.8 %bitcast_dynamic-update-slice_fusion.2 = (bf16[2,256,512]{2,1,0:T(8,128)(2,1)S(1)}, bf16[256,512]{1,0:T(8,128)(2,1)S(1)}) fusion(bf16[2,256,512]{2,1,0:T(8,128)(2,1)S(1)} %copy-done.6, s32[]{:T(128)S(6)} %min.27, f32[256,512]{1,0:T(8,128)S(1)} %get-tuple-element.635, bf16[1,2048,512]{2,1,0:T(8,128)(2,1)} %get-tuple-element.688, ...), kind=kOutput, calls=%fused_computation.101.clone.1 | convolution fusion | flops 1108475904 | bytes 5769220 | tf_op jit(solution)/shard_map/while/body/eval_jaxpr/dot_general | solution.py:113
  132.4 1.5 %collective-permute-start.2 = (bf16[256,512]{1,0:T(8,128)(2,1)S(1)}, bf16[256,512]{1,0:T(8,128)(2,1)S(1)}, u32[]{:S(2)}, u32[]{:S(2)}) collective-permute-start(bf16[256,512]{1,0:T(8,128)(2,1)S(1)} %get-tuple-element.637), channel_id=1, source_target_pairs={{0,16},{1,17},{2,18},{3,19},{4,20},{5,21},{6,22},{7,23},{8,24},{9,... | collective-permute-start | bytes 786440 | tf_op jit(solution)/shard_map/while/body/eval_jaxpr/ppermute | solution.py:33
  135.0 3.5 %all-to-all-start = ((bf16[2,256,512]{2,1,0:T(8,128)(2,1)}), bf16[2,256,512]{2,1,0:T(8,128)(2,1)S(1)}, u32[]{:S(2)}, u32[]{:S(2)}) async-start(bf16[2,256,512]{2,1,0:T(8,128)(2,1)} %get-tuple-element.409), calls=%async_computation | async-start | bytes 1048576 | tf_op jit(solution)/shard_map/all_to_all | solution.py:136
  (192 shorter events, 57.8 us)
Async XLA Ops:
  4.0 9.4 %copy-start.9 = (s32[2,16]{1,0:T(2,128)S(1)}, s32[2,16]{1,0:T(2,128)}, u32[]{:S(2)}) copy-start(s32[2,16]{1,0:T(2,128)} %get-tuple-element.685) | copy-start | bytes 388 | tf_op jit(solution)/shard_map/while
  4.0 9.4 %copy-start.8 = (s32[2,2,3]{2,1,0:T(2,128)S(1)}, s32[2,2,3]{2,1,0:T(2,128)}, u32[]{:S(2)}) copy-start(s32[2,2,3]{2,1,0:T(2,128)} %get-tuple-element.683) | copy-start | bytes 148 | tf_op jit(solution)/shard_map/while
  4.0 10.2 %copy-start.10 = (bf16[1,512,1536]{2,1,0:T(8,128)(2,1)S(1)}, bf16[1,512,1536]{2,1,0:T(8,128)(2,1)}, u32[]{:S(2)}) copy-start(bf16[1,512,1536]{2,1,0:T(8,128)(2,1)} %get-tuple-element.682) | copy-start | bytes 4718596 | tf_op jit(solution)/shard_map/while
  5.7 12.1 %collective-permute-start.1 = (bf16[256,512]{1,0:T(8,128)(2,1)S(1)}, bf16[256,512]{1,0:T(8,128)(2,1)S(1)}, u32[]{:S(2)}, u32[]{:S(2)}) collective-permute-start(bf16[256,512]{1,0:T(8,128)(2,1)S(1)} %fusion.177), channel_id=1, source_target_pairs={{0,1},{1,2},{2,3},{3,4},{4,5},{5,6},{6,7},{7,8},{8,9},{9,10},{10,1... | collective-permute-start | bytes 786440 | tf_op jit(solution)/shard_map/while/body/eval_jaxpr/ppermute | solution.py:21
  9.1 13.4 %collective-permute-start = (bf16[256,512]{1,0:T(8,128)(2,1)S(1)}, bf16[256,512]{1,0:T(8,128)(2,1)S(1)}, u32[]{:S(2)}, u32[]{:S(2)}) collective-permute-start(bf16[256,512]{1,0:T(8,128)(2,1)S(1)} %fusion.177), channel_id=1, source_target_pairs={{1,0},{2,1},{3,2},{4,3},{5,4},{6,5},{7,6},{8,7},{9,8},{10,9},{11,1... | collective-permute-start | bytes 786440 | tf_op jit(solution)/shard_map/while/body/eval_jaxpr/ppermute | solution.py:23
  36.5 10.3 %copy-start.5 = (bf16[2,256,512]{2,1,0:T(8,128)(2,1)S(1)}, bf16[2,256,512]{2,1,0:T(8,128)(2,1)}, u32[]{:S(2)}) copy-start(bf16[2,256,512]{2,1,0:T(8,128)(2,1)} %copy-done.4) | copy-start | bytes 1572868 | tf_op jit(solution)/shard_map/while
  44.3 2.4 %collective-permute-start.2 = (bf16[256,512]{1,0:T(8,128)(2,1)S(1)}, bf16[256,512]{1,0:T(8,128)(2,1)S(1)}, u32[]{:S(2)}, u32[]{:S(2)}) collective-permute-start(bf16[256,512]{1,0:T(8,128)(2,1)S(1)} %get-tuple-element.637), channel_id=1, source_target_pairs={{0,16},{1,17},{2,18},{3,19},{4,20},{5,21},{6,22},{7,23},{8,24},{9,... | collective-permute-start | bytes 786440 | tf_op jit(solution)/shard_map/while/body/eval_jaxpr/ppermute | solution.py:33
  47.5 9.4 %copy-start.9 = (s32[2,16]{1,0:T(2,128)S(1)}, s32[2,16]{1,0:T(2,128)}, u32[]{:S(2)}) copy-start(s32[2,16]{1,0:T(2,128)} %get-tuple-element.685) | copy-start | bytes 388 | tf_op jit(solution)/shard_map/while
  47.5 9.4 %copy-start.8 = (s32[2,2,3]{2,1,0:T(2,128)S(1)}, s32[2,2,3]{2,1,0:T(2,128)}, u32[]{:S(2)}) copy-start(s32[2,2,3]{2,1,0:T(2,128)} %get-tuple-element.683) | copy-start | bytes 148 | tf_op jit(solution)/shard_map/while
  47.5 10.3 %copy-start.10 = (bf16[1,512,1536]{2,1,0:T(8,128)(2,1)S(1)}, bf16[1,512,1536]{2,1,0:T(8,128)(2,1)}, u32[]{:S(2)}) copy-start(bf16[1,512,1536]{2,1,0:T(8,128)(2,1)} %get-tuple-element.682) | copy-start | bytes 4718596 | tf_op jit(solution)/shard_map/while
  49.2 12.4 %collective-permute-start.1 = (bf16[256,512]{1,0:T(8,128)(2,1)S(1)}, bf16[256,512]{1,0:T(8,128)(2,1)S(1)}, u32[]{:S(2)}, u32[]{:S(2)}) collective-permute-start(bf16[256,512]{1,0:T(8,128)(2,1)S(1)} %fusion.177), channel_id=1, source_target_pairs={{0,1},{1,2},{2,3},{3,4},{4,5},{5,6},{6,7},{7,8},{8,9},{9,10},{10,1... | collective-permute-start | bytes 786440 | tf_op jit(solution)/shard_map/while/body/eval_jaxpr/ppermute | solution.py:21
  52.7 14.1 %collective-permute-start = (bf16[256,512]{1,0:T(8,128)(2,1)S(1)}, bf16[256,512]{1,0:T(8,128)(2,1)S(1)}, u32[]{:S(2)}, u32[]{:S(2)}) collective-permute-start(bf16[256,512]{1,0:T(8,128)(2,1)S(1)} %fusion.177), channel_id=1, source_target_pairs={{1,0},{2,1},{3,2},{4,3},{5,4},{6,5},{7,6},{8,7},{9,8},{10,9},{11,1... | collective-permute-start | bytes 786440 | tf_op jit(solution)/shard_map/while/body/eval_jaxpr/ppermute | solution.py:23
  80.8 10.5 %copy-start.5 = (bf16[2,256,512]{2,1,0:T(8,128)(2,1)S(1)}, bf16[2,256,512]{2,1,0:T(8,128)(2,1)}, u32[]{:S(2)}) copy-start(bf16[2,256,512]{2,1,0:T(8,128)(2,1)} %copy-done.4) | copy-start | bytes 1572868 | tf_op jit(solution)/shard_map/while
  88.6 2.6 %copy-start.7 = (bf16[2,256,512]{2,1,0:T(8,128)(2,1)}, bf16[2,256,512]{2,1,0:T(8,128)(2,1)S(1)}, u32[]{:S(2)}) copy-start(bf16[2,256,512]{2,1,0:T(8,128)(2,1)S(1)} %get-tuple-element.677) | copy-start | bytes 1572868 | tf_op jit(solution)/shard_map/while
  88.6 2.6 %collective-permute-start.2 = (bf16[256,512]{1,0:T(8,128)(2,1)S(1)}, bf16[256,512]{1,0:T(8,128)(2,1)S(1)}, u32[]{:S(2)}, u32[]{:S(2)}) collective-permute-start(bf16[256,512]{1,0:T(8,128)(2,1)S(1)} %get-tuple-element.637), channel_id=1, source_target_pairs={{0,16},{1,17},{2,18},{3,19},{4,20},{5,21},{6,22},{7,23},{8,24},{9,... | collective-permute-start | bytes 786440 | tf_op jit(solution)/shard_map/while/body/eval_jaxpr/ppermute | solution.py:33
  91.9 9.4 %copy-start.9 = (s32[2,16]{1,0:T(2,128)S(1)}, s32[2,16]{1,0:T(2,128)}, u32[]{:S(2)}) copy-start(s32[2,16]{1,0:T(2,128)} %get-tuple-element.685) | copy-start | bytes 388 | tf_op jit(solution)/shard_map/while
  91.9 9.4 %copy-start.8 = (s32[2,2,3]{2,1,0:T(2,128)S(1)}, s32[2,2,3]{2,1,0:T(2,128)}, u32[]{:S(2)}) copy-start(s32[2,2,3]{2,1,0:T(2,128)} %get-tuple-element.683) | copy-start | bytes 148 | tf_op jit(solution)/shard_map/while
  92.0 10.3 %copy-start.10 = (bf16[1,512,1536]{2,1,0:T(8,128)(2,1)S(1)}, bf16[1,512,1536]{2,1,0:T(8,128)(2,1)}, u32[]{:S(2)}) copy-start(bf16[1,512,1536]{2,1,0:T(8,128)(2,1)} %get-tuple-element.682) | copy-start | bytes 4718596 | tf_op jit(solution)/shard_map/while
  93.7 12.4 %collective-permute-start.1 = (bf16[256,512]{1,0:T(8,128)(2,1)S(1)}, bf16[256,512]{1,0:T(8,128)(2,1)S(1)}, u32[]{:S(2)}, u32[]{:S(2)}) collective-permute-start(bf16[256,512]{1,0:T(8,128)(2,1)S(1)} %fusion.177), channel_id=1, source_target_pairs={{0,1},{1,2},{2,3},{3,4},{4,5},{5,6},{6,7},{7,8},{8,9},{9,10},{10,1... | collective-permute-start | bytes 786440 | tf_op jit(solution)/shard_map/while/body/eval_jaxpr/ppermute | solution.py:21
  96.1 14.5 %collective-permute-start = (bf16[256,512]{1,0:T(8,128)(2,1)S(1)}, bf16[256,512]{1,0:T(8,128)(2,1)S(1)}, u32[]{:S(2)}, u32[]{:S(2)}) collective-permute-start(bf16[256,512]{1,0:T(8,128)(2,1)S(1)} %fusion.177), channel_id=1, source_target_pairs={{1,0},{2,1},{3,2},{4,3},{5,4},{6,5},{7,6},{8,7},{9,8},{10,9},{11,1... | collective-permute-start | bytes 786440 | tf_op jit(solution)/shard_map/while/body/eval_jaxpr/ppermute | solution.py:23
  124.6 10.5 %copy-start.5 = (bf16[2,256,512]{2,1,0:T(8,128)(2,1)S(1)}, bf16[2,256,512]{2,1,0:T(8,128)(2,1)}, u32[]{:S(2)}) copy-start(bf16[2,256,512]{2,1,0:T(8,128)(2,1)} %copy-done.4) | copy-start | bytes 1572868 | tf_op jit(solution)/shard_map/while
  132.4 2.6 %copy-start.7 = (bf16[2,256,512]{2,1,0:T(8,128)(2,1)}, bf16[2,256,512]{2,1,0:T(8,128)(2,1)S(1)}, u32[]{:S(2)}) copy-start(bf16[2,256,512]{2,1,0:T(8,128)(2,1)S(1)} %get-tuple-element.677) | copy-start | bytes 1572868 | tf_op jit(solution)/shard_map/while
  132.4 2.6 %collective-permute-start.2 = (bf16[256,512]{1,0:T(8,128)(2,1)S(1)}, bf16[256,512]{1,0:T(8,128)(2,1)S(1)}, u32[]{:S(2)}, u32[]{:S(2)}) collective-permute-start(bf16[256,512]{1,0:T(8,128)(2,1)S(1)} %get-tuple-element.637), channel_id=1, source_target_pairs={{0,16},{1,17},{2,18},{3,19},{4,20},{5,21},{6,22},{7,23},{8,24},{9,... | collective-permute-start | bytes 786440 | tf_op jit(solution)/shard_map/while/body/eval_jaxpr/ppermute | solution.py:33
  135.0 5.4 %all-to-all-start = ((bf16[2,256,512]{2,1,0:T(8,128)(2,1)}), bf16[2,256,512]{2,1,0:T(8,128)(2,1)S(1)}, u32[]{:S(2)}, u32[]{:S(2)}) async-start(bf16[2,256,512]{2,1,0:T(8,128)(2,1)} %get-tuple-element.409), calls=%async_computation | async-start | bytes 1048576 | tf_op jit(solution)/shard_map/all_to_all | solution.py:136
  (19 other events, 28.3 us)
where the time goes:
time: 143 us; the launch traced here: 141 us
  local copies, waits for them, and re-layouts  39.6 us (28%)
  matrix products  32.9 us (23%)
  starting transfers between devices  30.7 us (21%)
  waiting for transfers between devices  25 us (17%)
  other arithmetic  9.64 us (7%)
  blocking collectives  2.38 us (2%)
    dot_general x3, matrix products, run_block(): jnp.dot(hidden, w_down[0], preferred_element_type=jnp.float32)  23.5 us
    ppermute x3, waiting for transfers between devices, with_halo(): lax.ppermute(head, axis, [((i + 1) % count, i) for i in range(ends)])  14.4 us
    ppermute x3, starting transfers between devices, with_halo(): lax.ppermute(head, axis, [((i + 1) % count, i) for i in range(ends)])  13.7 us
    ppermute x3, starting transfers between devices, with_halo(): lax.ppermute(tail, axis, [(i, (i + 1) % count) for i in range(ends)])  9.27 us
    ppermute x3, waiting for transfers between devices, with_halo(): lax.ppermute(tail, axis, [(i, (i + 1) % count) for i in range(ends)])  7.2 us
    reshape x6, local copies, waits for them, and re-layouts, attend(): near_values.reshape(-1, patch_rows, HEADS, head_width)[local_links]  5.29 us
    reshape x6, local copies, waits for them, and re-layouts, attend(): key_part = near_keys.reshape(-1, patch_rows, HEADS, head_width)[local_links]  5.29 us
    reshape x3, local copies, waits for them, and re-layouts, attend(): key_part.reshape(patch_count, links_count * patch_rows, HEADS, head_width)  4.35 us
  transfers between devices with their start and end apart: 10, of which 9 were waited for; matrix products, arithmetic and copies ran while one was open for 6% of the time, Pallas kernels for 0%

commit v1 on v0

v1 whole, which is shorter than its diff:
```python
import functools

import jax
import jax.numpy as jnp
from jax import lax
from jax.experimental import pallas as pl
from jax.experimental.pallas import tpu as pltpu
from jax.sharding import PartitionSpec as P

HEADS = 8
REACH = 2
FF_PARTS = 4
LANES = 128
epsilon = 1e-05
MESH = pl.DeviceIdType.MESH


def product(left, right):
    return jnp.dot(left, right, preferred_element_type=jnp.float32)


def normalize(values):
    center = jnp.mean(values, axis=-1, keepdims=True)
    moved = values - center
    spread = jnp.mean(moved * moved, axis=-1, keepdims=True)
    return (moved * lax.rsqrt(spread + epsilon)).astype(jnp.bfloat16)


def gelu(values):
    return 0.5 * values * (1.0 + lax.erf(values * (0.5**0.5)))


def kernel(
    segments,
    regions,
    links_ref,
    counts_ref,
    hits_ref,
    order_ref,
    wqkv_hbm,
    wout_hbm,
    wup_hbm,
    wdown_hbm,
    out_ref,
    wqkv,
    wout,
    wup,
    wdown,
    state,
    normed,
    queries,
    keys,
    values,
    attended,
    weight_sems,
    weight_send_sems,
    halo_sems,
    halo_send_sems,
):
    section = lax.axis_index("section")
    region = lax.axis_index("region")
    rows, width = state.shape
    patches = links_ref.shape[1]
    links_count = links_ref.shape[2]
    patch_rows = rows // patches
    margin = REACH * patch_rows
    head_width = width // HEADS
    group = LANES // head_width
    ff_part = wup.shape[2] // FF_PARTS
    has_left = region > 0
    has_right = region < regions - 1
    others = [lax.rem(section + i, segments) for i in range(1, segments)]

    barrier = pltpu.get_barrier_semaphore()
    for other in others:
        pl.semaphore_signal(barrier, inc=1, device_id={"section": other}, device_id_type=MESH)

    @pl.when(has_left)
    def _():
        pl.semaphore_signal(barrier, inc=1, device_id={"region": region - 1}, device_id_type=MESH)

    @pl.when(has_right)
    def _():
        pl.semaphore_signal(barrier, inc=1, device_id={"region": region + 1}, device_id_type=MESH)

    def weight_pieces(block):
        pieces = [(wqkv_hbm.at[0], wqkv.at[block]), (wout_hbm.at[0], wout.at[block])]
        for part in range(FF_PARTS):
            span = pl.ds(part * ff_part, ff_part)
            pieces.append((wup_hbm.at[0, :, span], wup.at[block, :, span]))
            pieces.append((wdown_hbm.at[0, span, :], wdown.at[block, span, :]))
        return pieces

    own_pieces = weight_pieces(section)
    piece_count = len(own_pieces)
    for i, (source, target) in enumerate(own_pieces):
        pltpu.make_async_copy(source, target, weight_sems.at[section, i]).start()

    peers = segments - 1 + (region > 0).astype(jnp.int32) + (region < regions - 1).astype(jnp.int32)
    pl.semaphore_wait(barrier, peers)

    def weight_sends():
        sends = []
        for n, other in enumerate(others):
            for i, (source, target) in enumerate(own_pieces):
                sends.append(
                    pltpu.make_async_remote_copy(
                        src_ref=source,
                        dst_ref=target,
                        send_sem=weight_send_sems.at[n, i],
                        recv_sem=weight_sems.at[section, i],
                        device_id={"section": other},
                        device_id_type=MESH,
                    )
                )
        return sends

    for send in weight_sends():
        send.start()

    def wait_weight(block, i):
        target = weight_pieces(block)[i][1]
        pltpu.make_async_copy(target, target, weight_sems.at[block, i]).wait()

    def halo_send(block, way):
        source = margin if way == 0 else rows
        target = margin + rows if way == 0 else 0
        return pltpu.make_async_remote_copy(
            src_ref=normed.at[block, pl.ds(source, margin)],
            dst_ref=normed.at[block, pl.ds(target, margin)],
            send_sem=halo_send_sems.at[block, way],
            recv_sem=halo_sems.at[block, way],
            device_id={"region": region - 1 if way == 0 else region + 1},
            device_id_type=MESH,
        )

    slots = lax.broadcasted_iota(jnp.int32, (rows, rows), 0)
    picks = (slots == order_ref[section]).astype(jnp.float32).astype(jnp.bfloat16)
    state[...] = lax.dot_general(
        picks, hits_ref[0], (((0,), (0,)), ((), ())), preferred_element_type=jnp.float32
    )
    lane = lax.broadcasted_iota(jnp.int32, (1, LANES), 1)
    head_lanes = [lane // head_width == j for j in range(group)]
    key_slot = lax.broadcasted_iota(jnp.int32, (1, patch_rows), 1)
    ones = jnp.ones((links_count * patch_rows, LANES), jnp.bfloat16)

    def near_pair(block, start, count):
        both = product(
            normed[block, pl.ds(start, count), :], wqkv[block, :, pl.ds(width, 2 * width)]
        ).astype(jnp.bfloat16)
        first = start // patch_rows
        for i in range(count // patch_rows):
            piece = both[i * patch_rows : (i + 1) * patch_rows]
            keys[first + i] = piece[:, :width]
            values[first + i] = piece[:, width:]

    def run_block(block, carry):
        normed[block, pl.ds(margin, rows), :] = normalize(state[...])

        @pl.when(has_left)
        def _():
            halo_send(block, 0).start()

        @pl.when(has_right)
        def _():
            halo_send(block, 1).start()

        wait_weight(block, 0)
        queries[...] = (
            product(normed[block, pl.ds(margin, rows), :], wqkv[block, :, pl.ds(0, width)])
            .astype(jnp.bfloat16)
            * head_width ** (-0.5)
        ).astype(jnp.bfloat16)
        near_pair(block, margin, rows)

        @pl.when(has_left)
        def _():
            halo_send(block, 1).wait_recv()

        @pl.when(has_right)
        def _():
            halo_send(block, 0).wait_recv()

        @pl.when(jnp.logical_not(has_left))
        def _():
            normed[block, pl.ds(0, margin), :] = jnp.zeros((margin, width), jnp.bfloat16)

        @pl.when(jnp.logical_not(has_right))
        def _():
            normed[block, pl.ds(margin + rows, margin), :] = jnp.zeros((margin, width), jnp.bfloat16)

        near_pair(block, 0, margin)
        near_pair(block, margin + rows, margin)

        for patch in range(patches):
            linked = [links_ref[section, patch, j] for j in range(links_count)]
            near = [
                jnp.clip(link - region * patches + REACH, 0, keys.shape[0] - 1) for link in linked
            ]
            mask = jnp.concatenate(
                [
                    key_slot < counts_ref[section, link // patches] - lax.rem(link, patches) * patch_rows
                    for link in linked
                ],
                axis=1,
            )
            span = pl.ds(patch * patch_rows, patch_rows)
            for first in range(0, width, LANES):
                columns = pl.ds(first, LANES)
                own = queries[span, columns]
                stacked = jnp.concatenate(
                    [jnp.where(chosen, own, jnp.zeros_like(own)) for chosen in head_lanes], axis=0
                )
                near_keys = jnp.concatenate([keys[i, :, columns] for i in near], axis=0)
                near_values = jnp.concatenate([values[i, :, columns] for i in near], axis=0)
                scores = lax.dot_general(
                    stacked, near_keys, (((1,), (1,)), ((), ())), preferred_element_type=jnp.float32
                )
                scores = jnp.where(mask, scores, -1e30)
                weights = jnp.exp(scores - jnp.max(scores, axis=-1, keepdims=True)).astype(jnp.bfloat16)
                mixed = product(weights, jnp.concatenate([near_values, ones], axis=1))
                mixed = mixed[:, :LANES] / mixed[:, LANES:]
                result = mixed[:patch_rows]
                for j in range(1, group):
                    result = jnp.where(
                        head_lanes[j], mixed[j * patch_rows : (j + 1) * patch_rows], result
                    )
                attended[span, columns] = result.astype(jnp.bfloat16)

        wait_weight(block, 1)
        middle = (state[...] + product(attended[...], wout[block])).astype(jnp.bfloat16)
        middle = middle.astype(jnp.float32)
        normed_mlp = normalize(middle)
        total = middle
        for part in range(FF_PARTS):
            span = pl.ds(part * ff_part, ff_part)
            wait_weight(block, 2 + 2 * part)
            hidden = gelu(product(normed_mlp, wup[block, :, span])).astype(jnp.bfloat16)
            wait_weight(block, 3 + 2 * part)
            total = total + product(hidden, wdown[block, span, :])
        state[...] = total.astype(jnp.bfloat16).astype(jnp.float32)

        @pl.when(has_left)
        def _():
            halo_send(block, 0).wait_send()

        @pl.when(has_right)
        def _():
            halo_send(block, 1).wait_send()

        return carry

    lax.fori_loop(0, segments, run_block, 0)
    out_ref[0] = state[...].astype(jnp.bfloat16)
    for send in weight_sends():
        send.wait_send()


def per_device(hits, order, links, counts, w_qkv, w_out, w_up, w_down):
    segments = lax.axis_size("section")
    regions = lax.axis_size("region")
    rows, width = hits.shape[1:]
    hidden = w_up.shape[2]
    patches = links.shape[1]
    patch_rows = rows // patches
    margin = REACH * patch_rows
    near_rows = rows + 2 * margin
    assert margin <= rows and w_qkv.shape[0] == 1
    piece_count = 2 + 2 * FF_PARTS
    vmem = pl.BlockSpec(memory_space=pltpu.VMEM)
    smem = pl.BlockSpec(memory_space=pltpu.SMEM)
    hbm = pl.BlockSpec(memory_space=pl.ANY)
    bf16 = jnp.bfloat16
    encoded = pl.pallas_call(
        functools.partial(kernel, segments, regions),
        out_shape=jax.ShapeDtypeStruct((1, rows, width), bf16),
        in_specs=[smem, smem, vmem, vmem, hbm, hbm, hbm, hbm],
        out_specs=vmem,
        scratch_shapes=[
            pltpu.VMEM((segments,) + w_qkv.shape[1:], bf16),
            pltpu.VMEM((segments,) + w_out.shape[1:], bf16),
            pltpu.VMEM((segments,) + w_up.shape[1:], bf16),
            pltpu.VMEM((segments,) + w_down.shape[1:], bf16),
            pltpu.VMEM((rows, width), jnp.float32),
            pltpu.VMEM((segments, near_rows, width), bf16),
            pltpu.VMEM((rows, width), bf16),
            pltpu.VMEM((near_rows // patch_rows, patch_rows, width), bf16),
            pltpu.VMEM((near_rows // patch_rows, patch_rows, width), bf16),
            pltpu.VMEM((rows, width), bf16),
            pltpu.SemaphoreType.DMA((segments, piece_count)),
            pltpu.SemaphoreType.DMA((segments - 1, piece_count)),
            pltpu.SemaphoreType.DMA((segments, 2)),
            pltpu.SemaphoreType.DMA((segments, 2)),
        ],
        compiler_params=pltpu.CompilerParams(
            collective_id=0, has_side_effects=True, vmem_limit_bytes=48 * 2**20
        ),
        name="blocks",
    )(links, counts, hits, order, w_qkv, w_out, w_up, w_down)
    own_count = counts[lax.axis_index("section"), lax.axis_index("region")]
    keep = jnp.arange(rows) < own_count
    return jnp.where(keep[None, :, None], encoded, jnp.zeros_like(encoded))


def solution(mesh):
    in_specs = (
        P("section", "region", None),
        P(None, "region", None),
        P(None, "region", None),
        P(),
        P("section", None, None),
        P("section", None, None),
        P("section", None, None),
        P("section", None, None),
    )
    out_specs = P("section", "region", None)
    return jax.shard_map(
        per_device, mesh=mesh, in_specs=in_specs, out_specs=out_specs, check_vma=False
    )
```

time: 143 us -> 49.5 us (0.35)
  the two profiles are of different devices: /device:TPU:24 before, /device:TPU:22 now
where the time goes in v1:
time: 49.5 us; the launch traced here: 49.2 us
  Pallas kernels  39.4 us (80%)
  local copies, waits for them, and re-layouts  8.29 us (17%)
  other arithmetic  1.46 us (3%)
    pallas_call x1, Pallas kernels, per_device(): pl.pallas_call(functools.partial(kernel, segments, regions), out_shape=ja...  39.4 us
    unnamed x14, local copies, waits for them, and re-layouts  7.02 us
    dynamic_slice x1, local copies, waits for them, and re-layouts, per_device(): own_count = counts[lax.axis_index('section'), lax.axis_index('region')]  1.26 us

profile of v1, /device:TPU:22, one launch (start us, length us, event | category | flops | bytes accessed | tf_op | source)
XLA Modules:
  0.0 49.2 jit_solution(2346815090133972719)
XLA Ops:
  0.0 1.3 %dynamic_slice.3 = s32[1,1]{1,0:T(1,128)} dynamic-slice(s32[2,16]{1,0:T(2,128)} %counts_ref.1, s32[]{:T(128)S(6)} %select_n.10, s32[]{:T(128)S(6)} %select_n.11), dynamic_slice_sizes={1,1} | dynamic-slice | bytes 12 | tf_op jit(solution)/shard_map/dynamic_slice | solution.py:300
  1.3 0.6 %iota_compare_fusion = pred[256]{0:T(512)(128)(4,1)S(1)} fusion(s32[]{:T(128)} %bitcast), kind=kLoop, calls=%fused_computation.1 | loop fusion | flops 256 | bytes 260 | tf_op jit(solution)/shard_map/lt | solution.py:301
  1.9 0.0 copy-start
  1.9 1.6 %copy-done = bf16[1,512,2048]{2,1,0:T(8,128)(2,1)S(1)} copy-done((bf16[1,512,2048]{2,1,0:T(8,128)(2,1)S(1)}, bf16[1,512,2048]{2,1,0:T(8,128)(2,1)}, u32[]{:S(2)}) %copy-start) | copy-done | bytes 2097176
  3.5 0.0 copy-start.1
  3.5 1.4 %copy-done.1 = bf16[1,512,1536]{2,1,0:T(8,128)(2,1)S(1)} copy-done((bf16[1,512,1536]{2,1,0:T(8,128)(2,1)S(1)}, bf16[1,512,1536]{2,1,0:T(8,128)(2,1)}, u32[]{:S(2)}) %copy-start.1) | copy-done | bytes 1572888
  4.9 0.0 copy-start.2
  4.9 1.0 %copy-done.2 = bf16[1,512,512]{2,1,0:T(8,128)(2,1)S(1)} copy-done((bf16[1,512,512]{2,1,0:T(8,128)(2,1)S(1)}, bf16[1,512,512]{2,1,0:T(8,128)(2,1)}, u32[]{:S(2)}) %copy-start.2) | copy-done | bytes 524312
  6.0 0.0 copy-start.3
  6.0 0.9 %copy-done.3 = bf16[1,256,512]{2,1,0:T(8,128)(2,1)S(1)} copy-done((bf16[1,256,512]{2,1,0:T(8,128)(2,1)S(1)}, bf16[1,256,512]{2,1,0:T(8,128)(2,1)}, u32[]{:S(2)}) %copy-start.3) | copy-done | bytes 262168
  6.9 0.0 copy-start.4
  6.9 0.7 %copy-done.4 = s32[2,16]{1,0:T(2,128)S(1)} copy-done((s32[2,16]{1,0:T(2,128)S(1)}, s32[2,16]{1,0:T(2,128)}, u32[]{:S(2)}) %copy-start.4) | copy-done | bytes 152
  7.6 0.0 copy-start.5
  7.6 0.7 %copy-done.5 = s32[2,2,3]{2,1,0:T(2,128)S(1)} copy-done((s32[2,2,3]{2,1,0:T(2,128)S(1)}, s32[2,2,3]{2,1,0:T(2,128)}, u32[]{:S(2)}) %copy-start.5) | copy-done | bytes 72
  8.3 0.0 copy-start.6
  8.3 0.7 %copy-done.6 = s32[2,1,256]{2,1,0:T(1,128)S(1)} copy-done((s32[2,1,256]{2,1,0:T(1,128)S(1)}, s32[2,1,256]{2,1,0:T(1,128)}, u32[]{:S(2)}) %copy-start.6) | copy-done | bytes 2072
  9.0 39.4 %blocks.1 = bf16[1,256,512]{2,1,0:T(8,128)(2,1)S(1)} custom-call(s32[2,2,3]{2,1,0:T(2,128)S(1)} %copy-done.5, s32[2,16]{1,0:T(2,128)S(1)} %copy-done.4, bf16[1,256,512]{2,1,0:T(8,128)(2,1)S(1)} %copy-done.3, s32[2,1,256]{2,1,0:T(1,128)S(1)} %copy-done.6, bf16[1,512,1536]{2,1,0:T(8,128)(2,1)S(1)} %copy-done.1, bf16[1,512,512]{2,1,0:T(8,128)(2,1)S(1)} %copy-done.2, ...), custom_call_target="tpu_custom_call" | custom-call | tf_op jit(solution)/shard_map/blocks/pallas_call | solution.py:274
  48.4 0.8 %broadcast_select_fusion = bf16[1,256,512]{2,1,0:T(8,128)(2,1)} fusion(bf16[1,256,512]{2,1,0:T(8,128)(2,1)S(1)} %blocks.1, pred[256]{0:T(512)(128)(4,1)S(1)} %iota_compare_fusion), kind=kLoop, calls=%fused_computation | loop fusion | flops 131072 | bytes 524544 | tf_op jit(solution)/shard_map/jit(_where)/select_n | solution.py:302
Async XLA Ops:
  1.9 1.6 %copy-start = (bf16[1,512,2048]{2,1,0:T(8,128)(2,1)S(1)}, bf16[1,512,2048]{2,1,0:T(8,128)(2,1)}, u32[]{:S(2)}) copy-start(bf16[1,512,2048]{2,1,0:T(8,128)(2,1)} %wup_hbm.1) | copy-start | bytes 6291460
  3.5 1.4 %copy-start.1 = (bf16[1,512,1536]{2,1,0:T(8,128)(2,1)S(1)}, bf16[1,512,1536]{2,1,0:T(8,128)(2,1)}, u32[]{:S(2)}) copy-start(bf16[1,512,1536]{2,1,0:T(8,128)(2,1)} %wqkv_hbm.1) | copy-start | bytes 4718596
  4.9 1.0 %copy-start.2 = (bf16[1,512,512]{2,1,0:T(8,128)(2,1)S(1)}, bf16[1,512,512]{2,1,0:T(8,128)(2,1)}, u32[]{:S(2)}) copy-start(bf16[1,512,512]{2,1,0:T(8,128)(2,1)} %wout_hbm.1) | copy-start | bytes 1572868
  6.0 0.9 %copy-start.3 = (bf16[1,256,512]{2,1,0:T(8,128)(2,1)S(1)}, bf16[1,256,512]{2,1,0:T(8,128)(2,1)}, u32[]{:S(2)}) copy-start(bf16[1,256,512]{2,1,0:T(8,128)(2,1)} %hits_ref.1) | copy-start | bytes 786436
  6.9 0.7 %copy-start.4 = (s32[2,16]{1,0:T(2,128)S(1)}, s32[2,16]{1,0:T(2,128)}, u32[]{:S(2)}) copy-start(s32[2,16]{1,0:T(2,128)} %counts_ref.1) | copy-start | bytes 388
  7.6 0.7 %copy-start.5 = (s32[2,2,3]{2,1,0:T(2,128)S(1)}, s32[2,2,3]{2,1,0:T(2,128)}, u32[]{:S(2)}) copy-start(s32[2,2,3]{2,1,0:T(2,128)} %links_ref.1) | copy-start | bytes 148
  8.3 0.7 %copy-start.6 = (s32[2,1,256]{2,1,0:T(1,128)S(1)}, s32[2,1,256]{2,1,0:T(1,128)}, u32[]{:S(2)}) copy-start(s32[2,1,256]{2,1,0:T(1,128)} %order_ref.1) | copy-start | bytes 6148

commit v2 on v1

--- a/solution.py
+++ b/solution.py
@@ -10,6 +10,7 @@
 HEADS = 8
 REACH = 2
 FF_PARTS = 4
+HALO_PARTS = 4
 LANES = 128
 epsilon = 1e-05
 MESH = pl.DeviceIdType.MESH
@@ -27,7 +28,14 @@
 
 
 def gelu(values):
-    return 0.5 * values * (1.0 + lax.erf(values * (0.5**0.5)))
+    size = jnp.abs(values)
+    t = pl.reciprocal(1.0 + (0.3275911 * 0.5**0.5) * size, approx=True)
+    series = 1.061405429 * t - 1.453152027
+    series = series * t + 1.421413741
+    series = series * t - 0.284496736
+    series = series * t + 0.254829592
+    tail = (series * t) * jnp.exp(-0.5 * (values * values))
+    return jnp.maximum(values, 0.0) - (0.5 * size) * tail
 
 
 def kernel(
@@ -63,25 +71,29 @@
     patches = links_ref.shape[1]
     links_count = links_ref.shape[2]
     patch_rows = rows // patches
-    margin = REACH * patch_rows
+    chunk = rows // HALO_PARTS
     head_width = width // HEADS
     group = LANES // head_width
     ff_part = wup.shape[2] // FF_PARTS
-    has_left = region > 0
-    has_right = region < regions - 1
+    parity = lax.rem(region, 2)
+    near_slot = 2 * (1 - parity)
+    far_slot = 2 * parity
+    buddy = region + 1 - 2 * parity
+    far_target = region + 2 - 4 * parity
+    far_source = region - 2 + 4 * parity
+    has_target = jnp.logical_and(far_target >= 0, far_target < regions)
+    has_source = jnp.logical_and(far_source >= 0, far_source < regions)
     others = [lax.rem(section + i, segments) for i in range(1, segments)]
 
     barrier = pltpu.get_barrier_semaphore()
     for other in others:
         pl.semaphore_signal(barrier, inc=1, device_id={"section": other}, device_id_type=MESH)
 
-    @pl.when(has_left)
+    pl.semaphore_signal(barrier, inc=1, device_id={"region": buddy}, device_id_type=MESH)
+
+    @pl.when(has_source)
     def _():
-        pl.semaphore_signal(barrier, inc=1, device_id={"region": region - 1}, device_id_type=MESH)
-
-    @pl.when(has_right)
-    def _():
-        pl.semaphore_signal(barrier, inc=1, device_id={"region": region + 1}, device_id_type=MESH)
+        pl.semaphore_signal(barrier, inc=1, device_id={"region": far_source}, device_id_type=MESH)
 
     def weight_pieces(block):
         pieces = [(wqkv_hbm.at[0], wqkv.at[block]), (wout_hbm.at[0], wout.at[block])]
@@ -96,7 +108,7 @@
     for i, (source, target) in enumerate(own_pieces):
         pltpu.make_async_copy(source, target, weight_sems.at[section, i]).start()
 
-    peers = segments - 1 + (region > 0).astype(jnp.int32) + (region < regions - 1).astype(jnp.int32)
+    peers = segments + has_target.astype(jnp.int32)
     pl.semaphore_wait(barrier, peers)
 
     def weight_sends():
@@ -122,15 +134,14 @@
         target = weight_pieces(block)[i][1]
         pltpu.make_async_copy(target, target, weight_sems.at[block, i]).wait()
 
-    def halo_send(block, way):
-        source = margin if way == 0 else rows
-        target = margin + rows if way == 0 else 0
+    def halo_send(block, way, part):
+        span = pl.ds(part * chunk, chunk)
         return pltpu.make_async_remote_copy(
-            src_ref=normed.at[block, pl.ds(source, margin)],
-            dst_ref=normed.at[block, pl.ds(target, margin)],
-            send_sem=halo_send_sems.at[block, way],
-            recv_sem=halo_sems.at[block, way],
-            device_id={"region": region - 1 if way == 0 else region + 1},
+            src_ref=normed.at[block, 1 if way == 0 else near_slot, span],
+            dst_ref=normed.at[block, far_slot, span],
+            send_sem=halo_send_sems.at[block, way, part],
+            recv_sem=halo_sems.at[block, way, part],
+            device_id={"region": buddy if way == 0 else far_target},
             device_id_type=MESH,
         )
 
@@ -144,53 +155,46 @@
     key_slot = lax.broadcasted_iota(jnp.int32, (1, patch_rows), 1)
     ones = jnp.ones((links_count * patch_rows, LANES), jnp.bfloat16)
 
-    def near_pair(block, start, count):
+    def near_pair(block, slot):
         both = product(
-            normed[block, pl.ds(start, count), :], wqkv[block, :, pl.ds(width, 2 * width)]
+            normed[block, slot], wqkv[block, :, pl.ds(width, 2 * width)]
         ).astype(jnp.bfloat16)
-        first = start // patch_rows
-        for i in range(count // patch_rows):
+        for i in range(patches):
             piece = both[i * patch_rows : (i + 1) * patch_rows]
-            keys[first + i] = piece[:, :width]
-            values[first + i] = piece[:, width:]
+            keys[slot * patches + i] = piece[:, :width]
+            values[slot * patches + i] = piece[:, width:]
 
     def run_block(block, carry):
-        normed[block, pl.ds(margin, rows), :] = normalize(state[...])
-
-        @pl.when(has_left)
-        def _():
-            halo_send(block, 0).start()
-
-        @pl.when(has_right)
-        def _():
-            halo_send(block, 1).start()
+        normed[block, 1] = normalize(state[...])
+        for part in range(HALO_PARTS):
+            halo_send(block, 0, part).start()
 
         wait_weight(block, 0)
         queries[...] = (
-            product(normed[block, pl.ds(margin, rows), :], wqkv[block, :, pl.ds(0, width)])
-            .astype(jnp.bfloat16)
+            product(normed[block, 1], wqkv[block, :, pl.ds(0, width)]).astype(jnp.bfloat16)
             * head_width ** (-0.5)
         ).astype(jnp.bfloat16)
-        near_pair(block, margin, rows)
-
-        @pl.when(has_left)
+        near_pair(block, 1)
+
+        for part in range(HALO_PARTS):
+            halo_send(block, 0, part).wait_recv()
+
+            @pl.when(has_target)
+            def _():
+                halo_send(block, 1, part).start()
+
+        near_pair(block, near_slot)
+
+        @pl.when(has_source)
         def _():
-            halo_send(block, 1).wait_recv()
-
-        @pl.when(has_right)
+            for part in range(HALO_PARTS):
+                halo_send(block, 1, part).wait_recv()
+
+        @pl.when(jnp.logical_not(has_source))
         def _():
-            halo_send(block, 0).wait_recv()
-
-        @pl.when(jnp.logical_not(has_left))
-        def _():
-            normed[block, pl.ds(0, margin), :] = jnp.zeros((margin, width), jnp.bfloat16)
-
-        @pl.when(jnp.logical_not(has_right))
-        def _():
-            normed[block, pl.ds(margin + rows, margin), :] = jnp.zeros((margin, width), jnp.bfloat16)
-
-        near_pair(block, 0, margin)
-        near_pair(block, margin + rows, margin)
+            normed[block, far_slot] = jnp.zeros((rows, width), jnp.bfloat16)
+
+        near_pair(block, far_slot)
 
         for patch in range(patches):
             linked = [links_ref[section, patch, j] for j in range(links_count)]
@@ -240,18 +244,20 @@
             total = total + product(hidden, wdown[block, span, :])
         state[...] = total.astype(jnp.bfloat16).astype(jnp.float32)
 
-        @pl.when(has_left)
+        for part in range(HALO_PARTS):
+            halo_send(block, 0, part).wait_send()
+
+        @pl.when(has_target)
         def _():
-            halo_send(block, 0).wait_send()
-
-        @pl.when(has_right)
-        def _():
-            halo_send(block, 1).wait_send()
+            for part in range(HALO_PARTS):
+                halo_send(block, 1, part).wait_send()
 
         return carry
 
     lax.fori_loop(0, segments, run_block, 0)
-    out_ref[0] = state[...].astype(jnp.bfloat16)
+    row = lax.broadcasted_iota(jnp.int32, (rows, 1), 0)
+    kept = jnp.where(row < counts_ref[section, region], state[...], 0.0)
+    out_ref[0] = kept.astype(jnp.bfloat16)
     for send in weight_sends():
         send.wait_send()
 
@@ -260,18 +266,16 @@
     segments = lax.axis_size("section")
     regions = lax.axis_size("region")
     rows, width = hits.shape[1:]
-    hidden = w_up.shape[2]
     patches = links.shape[1]
     patch_rows = rows // patches
-    margin = REACH * patch_rows
-    near_rows = rows + 2 * margin
-    assert margin <= rows and w_qkv.shape[0] == 1
+    near_patches = patches + 2 * REACH
+    assert patches == REACH and regions % 2 == 0 and w_qkv.shape[0] == 1
     piece_count = 2 + 2 * FF_PARTS
     vmem = pl.BlockSpec(memory_space=pltpu.VMEM)
     smem = pl.BlockSpec(memory_space=pltpu.SMEM)
-    hbm = pl.BlockSpec(memory_space=pl.ANY)
+    hbm = pl.BlockSpec(memory_space=pltpu.HBM)
     bf16 = jnp.bfloat16
-    encoded = pl.pallas_call(
+    return pl.pallas_call(
         functools.partial(kernel, segments, regions),
         out_shape=jax.ShapeDtypeStruct((1, rows, width), bf16),
         in_specs=[smem, smem, vmem, vmem, hbm, hbm, hbm, hbm],
@@ -282,24 +286,21 @@
             pltpu.VMEM((segments,) + w_up.shape[1:], bf16),
             pltpu.VMEM((segments,) + w_down.shape[1:], bf16),
             pltpu.VMEM((rows, width), jnp.float32),
-            pltpu.VMEM((segments, near_rows, width), bf16),
+            pltpu.VMEM((segments, 3, rows, width), bf16),
             pltpu.VMEM((rows, width), bf16),
-            pltpu.VMEM((near_rows // patch_rows, patch_rows, width), bf16),
-            pltpu.VMEM((near_rows // patch_rows, patch_rows, width), bf16),
+            pltpu.VMEM((near_patches, patch_rows, width), bf16),
+            pltpu.VMEM((near_patches, patch_rows, width), bf16),
             pltpu.VMEM((rows, width), bf16),
             pltpu.SemaphoreType.DMA((segments, piece_count)),
             pltpu.SemaphoreType.DMA((segments - 1, piece_count)),
-            pltpu.SemaphoreType.DMA((segments, 2)),
-            pltpu.SemaphoreType.DMA((segments, 2)),
+            pltpu.SemaphoreType.DMA((segments, 2, HALO_PARTS)),
+            pltpu.SemaphoreType.DMA((segments, 2, HALO_PARTS)),
         ],
         compiler_params=pltpu.CompilerParams(
-            collective_id=0, has_side_effects=True, vmem_limit_bytes=48 * 2**20
+            collective_id=0, has_side_effects=True, vmem_limit_bytes=60 * 2**20
         ),
         name="blocks",
     )(links, counts, hits, order, w_qkv, w_out, w_up, w_down)
-    own_count = counts[lax.axis_index("section"), lax.axis_index("region")]
-    keep = jnp.arange(rows) < own_count
-    return jnp.where(keep[None, :, None], encoded, jnp.zeros_like(encoded))
 
 
 def solution(mesh):

time: 49.5 us -> 41.9 us (0.85)
  the two profiles are of different devices: /device:TPU:22 before, /device:TPU:24 now
where the time goes in v2:
time: 41.9 us; the launch traced here: 41.8 us
  Pallas kernels  40.1 us (96%)
  local copies, waits for them, and re-layouts  1.67 us (4%)
    pallas_call x1, Pallas kernels, per_device(): pl.pallas_call(functools.partial(kernel, segments, regions), out_shape=ja...  40.1 us
    unnamed x1, local copies, waits for them, and re-layouts  1.67 us

profile of v2, /device:TPU:24, one launch (start us, length us, event | category | flops | bytes accessed | tf_op | source)
XLA Modules:
  0.0 41.8 jit_solution(1299755600230393298)
XLA Ops:
  0.0 40.1 %blocks.1 = bf16[1,256,512]{2,1,0:T(8,128)(2,1)} custom-call(s32[2,2,3]{2,1,0:T(2,128)} %links_ref.1, s32[2,16]{1,0:T(2,128)} %counts_ref.1, bf16[1,256,512]{2,1,0:T(8,128)(2,1)} %hits_ref.1, s32[2,1,256]{2,1,0:T(1,128)} %order_ref.1, bf16[1,512,1536]{2,1,0:T(8,128)(2,1)} %wqkv_hbm.1, bf16[1,512,512]{2,1,0:T(8,128)(2,1)} %wout_hbm.1, ...), custom_call_target="tpu_custom_call" | custom-call | tf_op jit(solution)/shard_map/blocks/pallas_call | solution.py:278
  40.1 1.7 %copy.10 = bf16[1,256,512]{2,1,0:T(8,128)(2,1)} copy(bf16[1,256,512]{2,1,0:T(8,128)(2,1)} %blocks.1) | data formatting | bytes 524288

commit v3 on v2

--- a/solution.py
+++ b/solution.py
@@ -1,4 +1,5 @@
 import functools
+import math
 
 import jax
 import jax.numpy as jnp
@@ -41,10 +42,10 @@
 def kernel(
     segments,
     regions,
-    links_ref,
-    counts_ref,
-    hits_ref,
-    order_ref,
+    links_hbm,
+    counts_hbm,
+    hits_hbm,
+    order_hbm,
     wqkv_hbm,
     wout_hbm,
     wup_hbm,
@@ -60,6 +61,11 @@
     keys,
     values,
     attended,
+    hits_ref,
+    order_ref,
+    links_ref,
+    counts_ref,
+    input_sems,
     weight_sems,
     weight_send_sems,
     halo_sems,
@@ -85,6 +91,14 @@
     has_source = jnp.logical_and(far_source >= 0, far_source < regions)
     others = [lax.rem(section + i, segments) for i in range(1, segments)]
 
+    hits_copy = pltpu.make_async_copy(hits_hbm.at[0], hits_ref, input_sems.at[0])
+    order_copy = pltpu.make_async_copy(order_hbm.at[section], order_ref, input_sems.at[1])
+    links_copy = pltpu.make_async_copy(links_hbm, links_ref, input_sems.at[2])
+    counts_copy = pltpu.make_async_copy(counts_hbm, counts_ref, input_sems.at[3])
+    hits_copy.start()
+    order_copy.start()
+    links_copy.start()
+    counts_copy.start()
     barrier = pltpu.get_barrier_semaphore()
     for other in others:
         pl.semaphore_signal(barrier, inc=1, device_id={"section": other}, device_id_type=MESH)
@@ -96,20 +110,17 @@
         pl.semaphore_signal(barrier, inc=1, device_id={"region": far_source}, device_id_type=MESH)
 
     def weight_pieces(block):
-        pieces = [(wqkv_hbm.at[0], wqkv.at[block]), (wout_hbm.at[0], wout.at[block])]
-        for part in range(FF_PARTS):
-            span = pl.ds(part * ff_part, ff_part)
-            pieces.append((wup_hbm.at[0, :, span], wup.at[block, :, span]))
-            pieces.append((wdown_hbm.at[0, span, :], wdown.at[block, span, :]))
+        pieces = [
+            (wqkv_hbm.at[0], wqkv.at[block]),
+            (wout_hbm.at[0], wout.at[block]),
+            (wup_hbm.at[0], wup.at[block]),
+            (wdown_hbm.at[0], wdown.at[block]),
+        ]
         return pieces
 
     own_pieces = weight_pieces(section)
-    piece_count = len(own_pieces)
     for i, (source, target) in enumerate(own_pieces):
         pltpu.make_async_copy(source, target, weight_sems.at[section, i]).start()
-
-    peers = segments + has_target.astype(jnp.int32)
-    pl.semaphore_wait(barrier, peers)
 
     def weight_sends():
         sends = []
@@ -127,9 +138,6 @@
                 )
         return sends
 
-    for send in weight_sends():
-        send.start()
-
     def wait_weight(block, i):
         target = weight_pieces(block)[i][1]
         pltpu.make_async_copy(target, target, weight_sems.at[block, i]).wait()
@@ -145,11 +153,23 @@
             device_id_type=MESH,
         )
 
+    order_copy.wait()
     slots = lax.broadcasted_iota(jnp.int32, (rows, rows), 0)
-    picks = (slots == order_ref[section]).astype(jnp.float32).astype(jnp.bfloat16)
-    state[...] = lax.dot_general(
-        picks, hits_ref[0], (((0,), (0,)), ((), ())), preferred_element_type=jnp.float32
+    picks = (slots == order_ref[...]).astype(jnp.float32).astype(jnp.bfloat16)
+    hits_copy.wait()
+    start = lax.dot_general(
+        picks, hits_ref[...], (((0,), (0,)), ((), ())), preferred_element_type=jnp.float32
     )
+    state[...] = start
+    normed[0, 1] = normalize(start)
+    links_copy.wait()
+    counts_copy.wait()
+    pl.semaphore_wait(barrier, segments + has_target.astype(jnp.int32))
+    for part in range(HALO_PARTS):
+        halo_send(0, 0, part).start()
+    for send in weight_sends():
+        send.start()
+
     lane = lax.broadcasted_iota(jnp.int32, (1, LANES), 1)
     head_lanes = [lane // head_width == j for j in range(group)]
     key_slot = lax.broadcasted_iota(jnp.int32, (1, patch_rows), 1)
@@ -165,14 +185,10 @@
             values[slot * patches + i] = piece[:, width:]
 
     def run_block(block, carry):
-        normed[block, 1] = normalize(state[...])
-        for part in range(HALO_PARTS):
-            halo_send(block, 0, part).start()
-
         wait_weight(block, 0)
         queries[...] = (
-            product(normed[block, 1], wqkv[block, :, pl.ds(0, width)]).astype(jnp.bfloat16)
-            * head_width ** (-0.5)
+            product(normed[block, 1], wqkv[block, :, pl.ds(0, width)])
+            * (math.log2(math.e) * head_width ** (-0.5))
         ).astype(jnp.bfloat16)
         near_pair(block, 1)
 
@@ -196,53 +212,78 @@
 
         near_pair(block, far_slot)
 
+        masks, nears = [], []
         for patch in range(patches):
             linked = [links_ref[section, patch, j] for j in range(links_count)]
-            near = [
-                jnp.clip(link - region * patches + REACH, 0, keys.shape[0] - 1) for link in linked
-            ]
-            mask = jnp.concatenate(
-                [
-                    key_slot < counts_ref[section, link // patches] - lax.rem(link, patches) * patch_rows
-                    for link in linked
-                ],
-                axis=1,
-            )
-            span = pl.ds(patch * patch_rows, patch_rows)
-            for first in range(0, width, LANES):
-                columns = pl.ds(first, LANES)
-                own = queries[span, columns]
-                stacked = jnp.concatenate(
-                    [jnp.where(chosen, own, jnp.zeros_like(own)) for chosen in head_lanes], axis=0
+            nears.append(
+                [jnp.clip(link - region * patches + REACH, 0, keys.shape[0] - 1) for link in linked]
+            )
+            masks.append(
+                jnp.concatenate(
+                    [
+                        key_slot
+                        < counts_ref[section, link // patches] - lax.rem(link, patches) * patch_rows
+                        for link in linked
+                    ],
+                    axis=1,
                 )
-                near_keys = jnp.concatenate([keys[i, :, columns] for i in near], axis=0)
-                near_values = jnp.concatenate([values[i, :, columns] for i in near], axis=0)
-                scores = lax.dot_general(
-                    stacked, near_keys, (((1,), (1,)), ((), ())), preferred_element_type=jnp.float32
+            )
+
+        def patch_scores(patch, first):
+            own = queries[pl.ds(patch * patch_rows, patch_rows), pl.ds(first, LANES)]
+            stacked = jnp.concatenate(
+                [jnp.where(chosen, own, jnp.zeros_like(own)) for chosen in head_lanes], axis=0
+            )
+            near_keys = jnp.concatenate(
+                [keys[i, :, pl.ds(first, LANES)] for i in nears[patch]], axis=0
+            )
+            return lax.dot_general(
+                stacked, near_keys, (((1,), (1,)), ((), ())), preferred_element_type=jnp.float32
+            )
+
+        steps = [(patch, first) for patch in range(patches) for first in range(0, width, LANES)]
+        ahead = patch_scores(*steps[0])
+        for n, (patch, first) in enumerate(steps):
+            scores = ahead
+            if n + 1 < len(steps):
+                ahead = patch_scores(*steps[n + 1])
+            scores = jnp.where(masks[patch], scores, -1e30)
+            weights = jnp.exp2(scores - jnp.max(scores, axis=-1, keepdims=True)).astype(jnp.bfloat16)
+            near_values = jnp.concatenate(
+                [values[i, :, pl.ds(first, LANES)] for i in nears[patch]], axis=0
+            )
+            mixed = product(weights, jnp.concatenate([near_values, ones], axis=1))
+            mixed = mixed[:, :LANES] * pl.reciprocal(mixed[:, LANES:], approx=True)
+            result = mixed[:patch_rows]
+            for j in range(1, group):
+                result = jnp.where(
+                    head_lanes[j], mixed[j * patch_rows : (j + 1) * patch_rows], result
                 )
-                scores = jnp.where(mask, scores, -1e30)
-                weights = jnp.exp(scores - jnp.max(scores, axis=-1, keepdims=True)).astype(jnp.bfloat16)
-                mixed = product(weights, jnp.concatenate([near_values, ones], axis=1))
-                mixed = mixed[:, :LANES] / mixed[:, LANES:]
-                result = mixed[:patch_rows]
-                for j in range(1, group):
-                    result = jnp.where(
-                        head_lanes[j], mixed[j * patch_rows : (j + 1) * patch_rows], result
-                    )
-                attended[span, columns] = result.astype(jnp.bfloat16)
-
-        wait_weight(block, 1)
+            attended[pl.ds(patch * patch_rows, patch_rows), pl.ds(first, LANES)] = result.astype(
+                jnp.bfloat16
+            )
+
+        for i in range(1, 4):
+            wait_weight(block, i)
         middle = (state[...] + product(attended[...], wout[block])).astype(jnp.bfloat16)
         middle = middle.astype(jnp.float32)
         normed_mlp = normalize(middle)
         total = middle
+        ahead = product(normed_mlp, wup[block, :, pl.ds(0, ff_part)])
         for part in range(FF_PARTS):
-            span = pl.ds(part * ff_part, ff_part)
-            wait_weight(block, 2 + 2 * part)
-            hidden = gelu(product(normed_mlp, wup[block, :, span])).astype(jnp.bfloat16)
-            wait_weight(block, 3 + 2 * part)
-            total = total + product(hidden, wdown[block, span, :])
-        state[...] = total.astype(jnp.bfloat16).astype(jnp.float32)
+            raised = ahead
+            if part + 1 < FF_PARTS:
+                ahead = product(normed_mlp, wup[block, :, pl.ds((part + 1) * ff_part, ff_part)])
+            hidden = gelu(raised).astype(jnp.bfloat16)
+            total = total + product(hidden, wdown[block, pl.ds(part * ff_part, ff_part), :])
+        total = total.astype(jnp.bfloat16).astype(jnp.float32)
+        state[...] = total
+
+        @pl.when(block < segments - 1)
+        def _():
+            normed[block + 1, 1] = normalize(state[...])
+            for part in range(HALO_PARTS):
+                halo_send(block + 1, 0, part).start()
 
         for part in range(HALO_PARTS):
             halo_send(block, 0, part).wait_send()
@@ -257,7 +298,7 @@
     lax.fori_loop(0, segments, run_block, 0)
     row = lax.broadcasted_iota(jnp.int32, (rows, 1), 0)
     kept = jnp.where(row < counts_ref[section, region], state[...], 0.0)
-    out_ref[0] = kept.astype(jnp.bfloat16)
+    out_ref[0] = kept
     for send in weight_sends():
         send.wait_send()
 
@@ -270,15 +311,14 @@
     patch_rows = rows // patches
     near_patches = patches + 2 * REACH
     assert patches == REACH and regions % 2 == 0 and w_qkv.shape[0] == 1
-    piece_count = 2 + 2 * FF_PARTS
+    piece_count = 4
     vmem = pl.BlockSpec(memory_space=pltpu.VMEM)
-    smem = pl.BlockSpec(memory_space=pltpu.SMEM)
     hbm = pl.BlockSpec(memory_space=pltpu.HBM)
     bf16 = jnp.bfloat16
-    return pl.pallas_call(
+    encoded = pl.pallas_call(
         functools.partial(kernel, segments, regions),
-        out_shape=jax.ShapeDtypeStruct((1, rows, width), bf16),
-        in_specs=[smem, smem, vmem, vmem, hbm, hbm, hbm, hbm],
+        out_shape=jax.ShapeDtypeStruct((1, rows, width), jnp.float32),
+        in_specs=[hbm] * 8,
         out_specs=vmem,
         scratch_shapes=[
             pltpu.VMEM((segments,) + w_qkv.shape[1:], bf16),
@@ -291,6 +331,11 @@
             pltpu.VMEM((near_patches, patch_rows, width), bf16),
             pltpu.VMEM((near_patches, patch_rows, width), bf16),
             pltpu.VMEM((rows, width), bf16),
+            pltpu.VMEM((rows, width), bf16),
+            pltpu.VMEM(order.shape[1:], jnp.int32),
+            pltpu.SMEM(links.shape, jnp.int32),
+            pltpu.SMEM(counts.shape, jnp.int32),
+            pltpu.SemaphoreType.DMA((4,)),
             pltpu.SemaphoreType.DMA((segments, piece_count)),
             pltpu.SemaphoreType.DMA((segments - 1, piece_count)),
             pltpu.SemaphoreType.DMA((segments, 2, HALO_PARTS)),
@@ -301,6 +346,7 @@
         ),
         name="blocks",
     )(links, counts, hits, order, w_qkv, w_out, w_up, w_down)
+    return encoded.astype(bf16)
 
 
 def solution(mesh):

time: 41.9 us -> 38.1 us (0.909)
  Pallas kernels: 40.1 us -> 36.1 us
  other arithmetic: 0 us -> 1.78 us
  local copies, waits for them, and re-layouts: 1.67 us -> 0 us
    pallas_call x1, Pallas kernels: 40.1 us -> 36.1 us  [per_device(): pl.pallas_call(functools.partial(kernel, segments, regions), out_shape=ja...]
    convert_element_type x0 -> x1, other arithmetic: none -> 1.78 us  [per_device(): return encoded.astype(bf16)]
    unnamed x1 -> x0, local copies, waits for them, and re-layouts: 1.67 us -> none
where the time goes in v3:
time: 38.1 us; the launch traced here: 37.9 us
  Pallas kernels  36.1 us (95%)
  other arithmetic  1.78 us (5%)
    pallas_call x1, Pallas kernels, per_device(): pl.pallas_call(functools.partial(kernel, segments, regions), out_shape=ja...  36.1 us
    convert_element_type x1, other arithmetic, per_device(): return encoded.astype(bf16)  1.78 us

profile of v3, /device:TPU:24, one launch (start us, length us, event | category | flops | bytes accessed | tf_op | source)
XLA Modules:
  0.0 37.9 jit_solution(10461751727201090030)
XLA Ops:
  0.0 36.1 %blocks.1 = f32[1,256,512]{2,1,0:T(8,128)} custom-call(s32[2,2,3]{2,1,0:T(2,128)} %links_hbm.1, s32[2,16]{1,0:T(2,128)} %counts_hbm.1, bf16[1,256,512]{2,1,0:T(8,128)(2,1)} %hits_hbm.1, s32[2,1,256]{2,1,0:T(1,128)} %order_hbm.1, bf16[1,512,1536]{2,1,0:T(8,128)(2,1)} %wqkv_hbm.1, bf16[1,512,512]{2,1,0:T(8,128)(2,1)} %wout_hbm.1, ...), custom_call_target="tpu_custom_call" | custom-call | tf_op jit(solution)/shard_map/blocks/pallas_call | solution.py:318
  36.1 1.8 %convert_element_type.3 = bf16[1,256,512]{2,1,0:T(8,128)(2,1)} convert(f32[1,256,512]{2,1,0:T(8,128)} %blocks.1) | non-fusion elementwise | flops 131072 | bytes 786432 | tf_op jit(solution)/shard_map/convert_element_type | solution.py:349

commit v4 on v3

--- a/solution.py
+++ b/solution.py
@@ -61,6 +61,8 @@
     keys,
     values,
     attended,
+    own_mixed,
+    own_highest,
     hits_ref,
     order_ref,
     links_ref,
@@ -174,6 +176,9 @@
     head_lanes = [lane // head_width == j for j in range(group)]
     key_slot = lax.broadcasted_iota(jnp.int32, (1, patch_rows), 1)
     ones = jnp.ones((links_count * patch_rows, LANES), jnp.bfloat16)
+    firsts = list(range(0, width, LANES))
+    last = segments - 1
+    per_patch = HALO_PARTS // patches
 
     def near_pair(block, slot):
         both = product(
@@ -184,88 +189,70 @@
             keys[slot * patches + i] = piece[:, :width]
             values[slot * patches + i] = piece[:, width:]
 
-    def run_block(block, carry):
-        wait_weight(block, 0)
-        queries[...] = (
-            product(normed[block, 1], wqkv[block, :, pl.ds(0, width)])
-            * (math.log2(math.e) * head_width ** (-0.5))
-        ).astype(jnp.bfloat16)
-        near_pair(block, 1)
-
-        for part in range(HALO_PARTS):
-            halo_send(block, 0, part).wait_recv()
-
-            @pl.when(has_target)
-            def _():
-                halo_send(block, 1, part).start()
-
-        near_pair(block, near_slot)
-
-        @pl.when(has_source)
-        def _():
-            for part in range(HALO_PARTS):
-                halo_send(block, 1, part).wait_recv()
-
-        @pl.when(jnp.logical_not(has_source))
-        def _():
-            normed[block, far_slot] = jnp.zeros((rows, width), jnp.bfloat16)
-
-        near_pair(block, far_slot)
-
-        masks, nears = [], []
-        for patch in range(patches):
-            linked = [links_ref[section, patch, j] for j in range(links_count)]
-            nears.append(
-                [jnp.clip(link - region * patches + REACH, 0, keys.shape[0] - 1) for link in linked]
-            )
-            masks.append(
-                jnp.concatenate(
-                    [
-                        key_slot
-                        < counts_ref[section, link // patches] - lax.rem(link, patches) * patch_rows
-                        for link in linked
-                    ],
-                    axis=1,
-                )
-            )
-
-        def patch_scores(patch, first):
-            own = queries[pl.ds(patch * patch_rows, patch_rows), pl.ds(first, LANES)]
-            stacked = jnp.concatenate(
-                [jnp.where(chosen, own, jnp.zeros_like(own)) for chosen in head_lanes], axis=0
-            )
-            near_keys = jnp.concatenate(
-                [keys[i, :, pl.ds(first, LANES)] for i in nears[patch]], axis=0
-            )
-            return lax.dot_general(
-                stacked, near_keys, (((1,), (1,)), ((), ())), preferred_element_type=jnp.float32
-            )
-
-        steps = [(patch, first) for patch in range(patches) for first in range(0, width, LANES)]
-        ahead = patch_scores(*steps[0])
-        for n, (patch, first) in enumerate(steps):
+    def key_mask(link):
+        kept = counts_ref[section, link // patches] - lax.rem(link, patches) * patch_rows
+        return key_slot < kept
+
+    own_masks, masks, nears = [], [], []
+    for patch in range(patches):
+        linked = [links_ref[section, patch, j] for j in range(1, links_count)]
+        nears.append(
+            [jnp.clip(link - region * patches + REACH, 0, keys.shape[0] - 1) for link in linked]
+        )
+        masks.append(jnp.concatenate([key_mask(link) for link in linked], axis=1))
+        own_masks.append(key_mask(region * patches + patch))
+
+    def scores_of(patch, first, near):
+        own = queries[pl.ds(patch * patch_rows, patch_rows), pl.ds(first, LANES)]
+        stacked = jnp.concatenate(
+            [jnp.where(chosen, own, jnp.zeros_like(own)) for chosen in head_lanes], axis=0
+        )
+        near_keys = jnp.concatenate([keys[i, :, pl.ds(first, LANES)] for i in near], axis=0)
+        return lax.dot_general(
+            stacked, near_keys, (((1,), (1,)), ((), ())), preferred_element_type=jnp.float32
+        )
+
+    def mix(weights, first, near):
+        near_values = jnp.concatenate([values[i, :, pl.ds(first, LANES)] for i in near], axis=0)
+        with_ones = jnp.concatenate([near_values, ones[: near_values.shape[0]]], axis=1)
+        return product(weights.astype(jnp.bfloat16), with_ones)
+
+    def attend_own(patch):
+        near = [patches + patch]
+        ahead = scores_of(patch, firsts[0], near)
+        for n, first in enumerate(firsts):
             scores = ahead
-            if n + 1 < len(steps):
-                ahead = patch_scores(*steps[n + 1])
+            if n + 1 < len(firsts):
+                ahead = scores_of(patch, firsts[n + 1], near)
+            scores = jnp.where(own_masks[patch], scores, -1e30)
+            highest = jnp.max(scores, axis=-1, keepdims=True)
+            own_highest[patch * len(firsts) + n] = highest
+            own_mixed[patch * len(firsts) + n] = mix(jnp.exp2(scores - highest), first, near)
+
+    def attend(patch):
+        near = nears[patch]
+        span = pl.ds(patch * patch_rows, patch_rows)
+        ahead = scores_of(patch, firsts[0], near)
+        for n, first in enumerate(firsts):
+            scores = ahead
+            if n + 1 < len(firsts):
+                ahead = scores_of(patch, firsts[n + 1], near)
             scores = jnp.where(masks[patch], scores, -1e30)
-            weights = jnp.exp2(scores - jnp.max(scores, axis=-1, keepdims=True)).astype(jnp.bfloat16)
-            near_values = jnp.concatenate(
-                [values[i, :, pl.ds(first, LANES)] for i in nears[patch]], axis=0
-            )
-            mixed = product(weights, jnp.concatenate([near_values, ones], axis=1))
+            before = own_highest[patch * len(firsts) + n]
+            highest = jnp.maximum(before, jnp.max(scores, axis=-1, keepdims=True))
+            mixed = mix(jnp.exp2(scores - highest), first, near)
+            mixed = mixed + own_mixed[patch * len(firsts) + n] * jnp.exp2(before - highest)
             mixed = mixed[:, :LANES] * pl.reciprocal(mixed[:, LANES:], approx=True)
             result = mixed[:patch_rows]
             for j in range(1, group):
                 result = jnp.where(
                     head_lanes[j], mixed[j * patch_rows : (j + 1) * patch_rows], result
                 )
-            attended[pl.ds(patch * patch_rows, patch_rows), pl.ds(first, LANES)] = result.astype(
-                jnp.bfloat16
-            )
-
-        for i in range(1, 4):
-            wait_weight(block, i)
-        middle = (state[...] + product(attended[...], wout[block])).astype(jnp.bfloat16)
+            attended[span, pl.ds(first, LANES)] = result.astype(jnp.bfloat16)
+
+    def feed_forward(block, start_row, count):
+        span = pl.ds(start_row, count)
+        middle = (state[span, :] + product(attended[span, :], wout[block])).astype(jnp.bfloat16)
         middle = middle.astype(jnp.float32)
         normed_mlp = normalize(middle)
         total = middle
@@ -276,15 +263,63 @@
                 ahead = product(normed_mlp, wup[block, :, pl.ds((part + 1) * ff_part, ff_part)])
             hidden = gelu(raised).astype(jnp.bfloat16)
             total = total + product(hidden, wdown[block, pl.ds(part * ff_part, ff_part), :])
-        total = total.astype(jnp.bfloat16).astype(jnp.float32)
-        state[...] = total
-
-        @pl.when(block < segments - 1)
+        return total.astype(jnp.bfloat16).astype(jnp.float32)
+
+    def pass_on(block, part):
+        halo_send(block, 0, part).wait_recv()
+
+        @pl.when(has_target)
         def _():
-            normed[block + 1, 1] = normalize(state[...])
+            halo_send(block, 1, part).start()
+
+    for block in range(segments):
+        first_parts = per_patch if block > 0 else 0
+        for part in range(first_parts):
+            pass_on(block, part)
+        wait_weight(block, 0)
+        queries[...] = (
+            product(normed[block, 1], wqkv[block, :, pl.ds(0, width)])
+            * (math.log2(math.e) * head_width ** (-0.5))
+        ).astype(jnp.bfloat16)
+        near_pair(block, 1)
+        later = list(range(first_parts, HALO_PARTS))
+        for patch in range(patches):
+            pass_on(block, later.pop(0))
+            attend_own(patch)
+        for part in later:
+            pass_on(block, part)
+        near_pair(block, near_slot)
+
+        @pl.when(has_source)
+        def _():
             for part in range(HALO_PARTS):
-                halo_send(block + 1, 0, part).start()
-
+                halo_send(block, 1, part).wait_recv()
+
+        @pl.when(jnp.logical_not(has_source))
+        def _():
+            normed[block, far_slot] = jnp.zeros((rows, width), jnp.bfloat16)
+
+        near_pair(block, far_slot)
+        for i in range(1, 4):
+            wait_weight(block, i)
+        if block < last:
+            for patch in range(patches):
+                attend(patch)
+                start_row = patch * patch_rows
+                total = feed_forward(block, start_row, patch_rows)
+                state[pl.ds(start_row, patch_rows), :] = total
+                normed[block + 1, 1, pl.ds(start_row, patch_rows), :] = normalize(total)
+                for part in range(patch * per_patch, (patch + 1) * per_patch):
+                    halo_send(block + 1, 0, part).start()
+        else:
+            for patch in range(patches):
+                attend(patch)
+            state[...] = feed_forward(block, 0, rows)
+
+    row = lax.broadcasted_iota(jnp.int32, (rows, 1), 0)
+    kept = jnp.where(row < counts_ref[section, region], state[...], 0.0)
+    out_ref[0] = kept
+    for block in range(segments):
         for part in range(HALO_PARTS):
             halo_send(block, 0, part).wait_send()
 
@@ -293,12 +328,6 @@
             for part in range(HALO_PARTS):
                 halo_send(block, 1, part).wait_send()
 
-        return carry
-
-    lax.fori_loop(0, segments, run_block, 0)
-    row = lax.broadcasted_iota(jnp.int32, (rows, 1), 0)
-    kept = jnp.where(row < counts_ref[section, region], state[...], 0.0)
-    out_ref[0] = kept
     for send in weight_sends():
         send.wait_send()
 
@@ -310,6 +339,7 @@
     patches = links.shape[1]
     patch_rows = rows // patches
     near_patches = patches + 2 * REACH
+    group = LANES * HEADS // width
     assert patches == REACH and regions % 2 == 0 and w_qkv.shape[0] == 1
     piece_count = 4
     vmem = pl.BlockSpec(memory_space=pltpu.VMEM)
@@ -331,6 +361,8 @@
             pltpu.VMEM((near_patches, patch_rows, width), bf16),
             pltpu.VMEM((near_patches, patch_rows, width), bf16),
             pltpu.VMEM((rows, width), bf16),
+            pltpu.VMEM((patches * (width // LANES), group * patch_rows, 2 * LANES), jnp.float32),
+            pltpu.VMEM((patches * (width // LANES), group * patch_rows, 1), jnp.float32),
             pltpu.VMEM((rows, width), bf16),
             pltpu.VMEM(order.shape[1:], jnp.int32),
             pltpu.SMEM(links.shape, jnp.int32),

time: 38.1 us -> 36.5 us (0.958)
  Pallas kernels: 36.1 us -> 34.4 us
    pallas_call x1, Pallas kernels: 36.1 us -> 34.4 us  [per_device(): pl.pallas_call(functools.partial(kernel, segments, regions), out_shape=ja...]
where the time goes in v4:
time: 36.5 us; the launch traced here: 36.2 us
  Pallas kernels  34.4 us (94%)
  other arithmetic  1.78 us (5%)
    pallas_call x1, Pallas kernels, per_device(): pl.pallas_call(functools.partial(kernel, segments, regions), out_shape=ja...  34.4 us
    convert_element_type x1, other arithmetic, per_device(): return encoded.astype(bf16)  1.78 us

profile of v4, /device:TPU:24, one launch (start us, length us, event | category | flops | bytes accessed | tf_op | source)
XLA Modules:
  0.0 36.2 jit_solution(15306159168565153908)
XLA Ops:
  0.0 34.4 %blocks.1 = f32[1,256,512]{2,1,0:T(8,128)} custom-call(s32[2,2,3]{2,1,0:T(2,128)} %links_hbm.1, s32[2,16]{1,0:T(2,128)} %counts_hbm.1, bf16[1,256,512]{2,1,0:T(8,128)(2,1)} %hits_hbm.1, s32[2,1,256]{2,1,0:T(1,128)} %order_hbm.1, bf16[1,512,1536]{2,1,0:T(8,128)(2,1)} %wqkv_hbm.1, bf16[1,512,512]{2,1,0:T(8,128)(2,1)} %wout_hbm.1, ...), custom_call_target="tpu_custom_call" | custom-call | tf_op jit(solution)/shard_map/blocks/pallas_call | solution.py:348
  34.4 1.8 %convert_element_type.3 = bf16[1,256,512]{2,1,0:T(8,128)(2,1)} convert(f32[1,256,512]{2,1,0:T(8,128)} %blocks.1) | non-fusion elementwise | flops 131072 | bytes 786432 | tf_op jit(solution)/shard_map/convert_element_type | solution.py:381

commit v5 on v4

--- a/solution.py
+++ b/solution.py
@@ -11,7 +11,7 @@
 HEADS = 8
 REACH = 2
 FF_PARTS = 4
-HALO_PARTS = 4
+HALO_PARTS = 8
 LANES = 128
 epsilon = 1e-05
 MESH = pl.DeviceIdType.MESH
@@ -180,14 +180,15 @@
     last = segments - 1
     per_patch = HALO_PARTS // patches
 
-    def near_pair(block, slot):
+    def near_pair(block, slot, first, count):
         both = product(
-            normed[block, slot], wqkv[block, :, pl.ds(width, 2 * width)]
+            normed[block, slot, pl.ds(first * patch_rows, count * patch_rows), :],
+            wqkv[block, :, pl.ds(width, 2 * width)],
         ).astype(jnp.bfloat16)
-        for i in range(patches):
+        for i in range(count):
             piece = both[i * patch_rows : (i + 1) * patch_rows]
-            keys[slot * patches + i] = piece[:, :width]
-            values[slot * patches + i] = piece[:, width:]
+            keys[slot * patches + first + i] = piece[:, :width]
+            values[slot * patches + first + i] = piece[:, width:]
 
     def key_mask(link):
         kept = counts_ref[section, link // patches] - lax.rem(link, patches) * patch_rows
@@ -281,25 +282,30 @@
             product(normed[block, 1], wqkv[block, :, pl.ds(0, width)])
             * (math.log2(math.e) * head_width ** (-0.5))
         ).astype(jnp.bfloat16)
-        near_pair(block, 1)
+        near_pair(block, 1, 0, patches)
         later = list(range(first_parts, HALO_PARTS))
+        turn = len(later) // (patches + 1)
         for patch in range(patches):
-            pass_on(block, later.pop(0))
+            for part in later[:turn]:
+                pass_on(block, part)
+            later = later[turn:]
             attend_own(patch)
         for part in later:
             pass_on(block, part)
-        near_pair(block, near_slot)
-
-        @pl.when(has_source)
-        def _():
-            for part in range(HALO_PARTS):
-                halo_send(block, 1, part).wait_recv()
+        near_pair(block, near_slot, 0, patches)
 
         @pl.when(jnp.logical_not(has_source))
         def _():
             normed[block, far_slot] = jnp.zeros((rows, width), jnp.bfloat16)
 
-        near_pair(block, far_slot)
+        for patch in range(patches):
+
+            @pl.when(has_source)
+            def _():
+                for part in range(patch * per_patch, (patch + 1) * per_patch):
+                    halo_send(block, 1, part).wait_recv()
+
+            near_pair(block, far_slot, patch, 1)
         for i in range(1, 4):
             wait_weight(block, i)
         if block < last:

time: 36.5 us -> 35.7 us (0.978)
  Pallas kernels: 34.4 us -> 33.7 us
    pallas_call x1, Pallas kernels: 34.4 us -> 33.7 us  [per_device(): pl.pallas_call(functools.partial(kernel, segments, regions), out_shape=ja...]
where the time goes in v5:
time: 35.7 us; the launch traced here: 35.5 us
  Pallas kernels  33.7 us (94%)
  other arithmetic  1.78 us (5%)
    pallas_call x1, Pallas kernels, per_device(): pl.pallas_call(functools.partial(kernel, segments, regions), out_shape=ja...  33.7 us
    convert_element_type x1, other arithmetic, per_device(): return encoded.astype(bf16)  1.78 us

profile of v5, /device:TPU:24, one launch (start us, length us, event | category | flops | bytes accessed | tf_op | source)
XLA Modules:
  0.0 35.5 jit_solution(18067188249150772338)
XLA Ops:
  0.0 33.7 %blocks.1 = f32[1,256,512]{2,1,0:T(8,128)} custom-call(s32[2,2,3]{2,1,0:T(2,128)} %links_hbm.1, s32[2,16]{1,0:T(2,128)} %counts_hbm.1, bf16[1,256,512]{2,1,0:T(8,128)(2,1)} %hits_hbm.1, s32[2,1,256]{2,1,0:T(1,128)} %order_hbm.1, bf16[1,512,1536]{2,1,0:T(8,128)(2,1)} %wqkv_hbm.1, bf16[1,512,512]{2,1,0:T(8,128)(2,1)} %wout_hbm.1, ...), custom_call_target="tpu_custom_call" | custom-call | tf_op jit(solution)/shard_map/blocks/pallas_call | solution.py:354
  33.7 1.8 %convert_element_type.3 = bf16[1,256,512]{2,1,0:T(8,128)(2,1)} convert(f32[1,256,512]{2,1,0:T(8,128)} %blocks.1) | non-fusion elementwise | flops 131072 | bytes 786432 | tf_op jit(solution)/shard_map/convert_element_type | solution.py:387

commit v6 on v5

--- a/solution.py
+++ b/solution.py
@@ -159,16 +159,22 @@
     slots = lax.broadcasted_iota(jnp.int32, (rows, rows), 0)
     picks = (slots == order_ref[...]).astype(jnp.float32).astype(jnp.bfloat16)
     hits_copy.wait()
-    start = lax.dot_general(
-        picks, hits_ref[...], (((0,), (0,)), ((), ())), preferred_element_type=jnp.float32
-    )
-    state[...] = start
-    normed[0, 1] = normalize(start)
-    links_copy.wait()
-    counts_copy.wait()
-    pl.semaphore_wait(barrier, segments + has_target.astype(jnp.int32))
-    for part in range(HALO_PARTS):
-        halo_send(0, 0, part).start()
+    for patch in range(patches):
+        span = pl.ds(patch * patch_rows, patch_rows)
+        start = lax.dot_general(
+            picks[:, patch * patch_rows : (patch + 1) * patch_rows],
+            hits_ref[...],
+            (((0,), (0,)), ((), ())),
+            preferred_element_type=jnp.float32,
+        )
+        state[span, :] = start
+        normed[0, 1, span, :] = normalize(start)
+        if patch == 0:
+            links_copy.wait()
+            counts_copy.wait()
+            pl.semaphore_wait(barrier, segments + has_target.astype(jnp.int32))
+        for part in range(patch * HALO_PARTS // patches, (patch + 1) * HALO_PARTS // patches):
+            halo_send(0, 0, part).start()
     for send in weight_sends():
         send.start()
 

time: 35.7 us -> 35.7 us (level)
  no operation moved by 1% of the time
where the time goes in v6:
time: 35.7 us; the launch traced here: 35.5 us
  Pallas kernels  33.8 us (95%)
  other arithmetic  1.78 us (5%)
    pallas_call x1, Pallas kernels, per_device(): pl.pallas_call(functools.partial(kernel, segments, regions), out_shape=ja...  33.8 us
    convert_element_type x1, other arithmetic, per_device(): return encoded.astype(bf16)  1.78 us

profile of v6, /device:TPU:24, one launch (start us, length us, event | category | flops | bytes accessed | tf_op | source)
XLA Modules:
  0.0 35.5 jit_solution(12261380648779537122)
XLA Ops:
  0.0 33.8 %blocks.1 = f32[1,256,512]{2,1,0:T(8,128)} custom-call(s32[2,2,3]{2,1,0:T(2,128)} %links_hbm.1, s32[2,16]{1,0:T(2,128)} %counts_hbm.1, bf16[1,256,512]{2,1,0:T(8,128)(2,1)} %hits_hbm.1, s32[2,1,256]{2,1,0:T(1,128)} %order_hbm.1, bf16[1,512,1536]{2,1,0:T(8,128)(2,1)} %wqkv_hbm.1, bf16[1,512,512]{2,1,0:T(8,128)(2,1)} %wout_hbm.1, ...), custom_call_target="tpu_custom_call" | custom-call | tf_op jit(solution)/shard_map/blocks/pallas_call | solution.py:360
  33.8 1.8 %convert_element_type.3 = bf16[1,256,512]{2,1,0:T(8,128)(2,1)} convert(f32[1,256,512]{2,1,0:T(8,128)} %blocks.1) | non-fusion elementwise | flops 131072 | bytes 786432 | tf_op jit(solution)/shard_map/convert_element_type | solution.py:393
